TPU v7x, 32 devices: a whole 2x2x4 slice. The times are simulated.
32 devices in a mesh: wide: 8 (over z, x), narrow: 4 (over y, core).
Axes of the slice: x: 2, y: 2, z: 4, core: 2. Of those that a mesh axis runs over, the one named last changes fastest.
Arguments:
- tokens: bfloat16 [2, 12288, 960], P(None, ('wide', 'narrow')), may hold values from -6 to 6
- lengths: int32 [2, 32, 8], P(None, ('wide', 'narrow')), may hold values from 0 to 384, as said below
- cotangent: bfloat16 [2, 12288, 960], P(None, ('wide', 'narrow')), may hold values from -6 to 6
- query_weight: bfloat16 [960, 960], P('wide', 'narrow'), may hold values from -0.25 to 0.25
- key_matrix: bfloat16 [960, 320], P('wide', 'narrow'), may hold values from -0.25 to 0.25
- value_matrix: bfloat16 [960, 320], P('wide', 'narrow'), may hold values from -0.1875 to 0.1875
- output_weight: bfloat16 [960, 960], P('wide', 'narrow'), may hold values from -0.5 to 0.5
- gate_weight: bfloat16 [960, 2560], P('narrow', 'wide'), may hold values from -0.1875 to 0.1875
- up_weight: bfloat16 [960, 2560], P('narrow', 'wide'), may hold values from -0.1875 to 0.1875
- down_weight: bfloat16 [2560, 960], P('wide', 'narrow'), may hold values from -0.25 to 0.25
- attention_gain: bfloat16 [960], P('narrow'), may hold values from 0.25 to 1.75
- feedforward_gain: bfloat16 [960], P('narrow'), may hold values from 0.25 to 1.75
Outputs:
- mixed: bfloat16 [2, 12288, 960], P(None, ('wide', 'narrow'))
- tokens_grad: bfloat16 [2, 12288, 960], P(None, ('wide', 'narrow'))
- query_grad: float32 [960, 960], P('wide', 'narrow')
- key_grad: float32 [960, 320], P('wide', 'narrow')
- value_grad: float32 [960, 320], P('wide', 'narrow')
- output_grad: float32 [960, 960], P('wide', 'narrow')
- gate_grad: float32 [960, 2560], P('narrow', 'wide')
- up_grad: float32 [960, 2560], P('narrow', 'wide')
- down_grad: float32 [2560, 960], P('wide', 'narrow')
- attention_gain_grad: float32 [960], P('narrow')
- feedforward_gain_grad: float32 [960], P('narrow')
Inputs may be any that keep to these rules, and one draw needn't show every extreme that they name: lengths[m, b] lists, in order, the documents packed into bucket b of micro-batch m; a bucket's lengths sum to at most 384, the rest of its rows are padding, zeros are empty slots, and in every draw some bucket holds a single document of 384 rows.
All inputs are finite; a program needn't handle non-finite values.
Results may differ from a plain program's by a relative error of at most 0.02.
Values may be sent and summed in bfloat16 or wider, within the bound.
No kernel may reach another device: no remote copies, remote signals or barrier semaphores. Data moves between devices by JAX's collectives and lax.ppermute only.
A program may use at most 256 MiB of HBM per device.

v0:
```python
import jax
import jax.numpy as jnp
from jax import lax
from jax.sharding import PartitionSpec as P

QUERY_HEADS = 15
KEY_VALUE_HEADS = 5
HEAD_WIDTH = 64


EPS = 1e-05
THETA = 10000.0


def segments_of(lengths_row, count_of_rows):
    ends = jnp.cumsum(lengths_row, dtype=jnp.int32)
    starts = ends - lengths_row
    places = jnp.arange(count_of_rows, dtype=jnp.int32)
    segment = jnp.sum((places[:, None] >= ends[None, :]).astype(jnp.int32), axis=1, dtype=jnp.int32)
    slot_ids = jnp.arange(lengths_row.shape[0], dtype=jnp.int32)
    opening = jnp.sum(
        jnp.where(segment[:, None] == slot_ids[None, :], starts[None, :], 0),
        axis=1,
        dtype=jnp.int32,
    )
    opening = jnp.where(segment == lengths_row.shape[0], ends[-1], opening)
    return (segment, places - opening)


def rotation_tables(position, head_size):
    half = head_size // 2
    freqs = THETA ** (-jnp.arange(half, dtype=jnp.float32) * 2.0 / head_size)
    angles = position.astype(jnp.float32)[:, None] * freqs[None, :]
    return (jnp.cos(angles)[:, None, :], jnp.sin(angles)[:, None, :])


def rotate(field, cosine_table, sine_table, head_size, inverse):
    count_of_rows = field.shape[0]
    pieces = field.reshape(count_of_rows, -1, head_size)
    half = head_size // 2
    left_half = pieces[..., :half]
    right_half = pieces[..., half:]
    sine_used = -sine_table if inverse else sine_table
    turned = jnp.concatenate(
        [
            left_half * cosine_table - right_half * sine_used,
            right_half * cosine_table + left_half * sine_used,
        ],
        axis=-1,
    )
    return turned.reshape(count_of_rows, -1)


def rms_scale(field):
    return lax.rsqrt(jnp.mean(field * field, axis=1, keepdims=True) + EPS)


def rms_back(field, scale, gain, upstream):
    normed = field * scale
    gain_grad = jnp.sum(upstream * normed, axis=0)
    normed_grad = upstream * gain
    field_grad = scale * (
        normed_grad - normed * jnp.mean(normed_grad * normed, axis=1, keepdims=True)
    )
    return (field_grad, gain_grad)


def head_block(matrix, member, width):
    return matrix[:, member * width : (member + 1) * width]


def masked_logits(queries, key_block, allowed, head_size):
    logits = jnp.einsum(
        "qcd,kd->cqk", queries, key_block, preferred_element_type=jnp.float32
    ) * head_size ** (-0.5)
    return jnp.where(allowed[None], logits, -1000000000.0)


def attention_forward(
    rotated_queries, rotated_keys, projected_values, allowed, head_size, heads_per_group
):
    count_of_rows = rotated_queries.shape[0]
    outputs = []
    log_sums = []
    for member in range(rotated_keys.shape[1] // head_size):
        queries = head_block(rotated_queries, member, heads_per_group * head_size).reshape(
            count_of_rows, heads_per_group, head_size
        )
        key_block = head_block(rotated_keys, member, head_size)
        value_block = head_block(projected_values, member, head_size)
        logits = masked_logits(queries, key_block, allowed, head_size)
        row_peak = jnp.max(logits, axis=-1, keepdims=True)
        shifted = jnp.exp(logits - row_peak)
        denominator = jnp.sum(shifted, axis=-1, keepdims=True)
        soft_probs = (shifted / denominator).astype(jnp.bfloat16)
        attended = jnp.einsum(
            "cqk,kd->qcd", soft_probs, value_block, preferred_element_type=jnp.float32
        )
        outputs.append(attended.reshape(count_of_rows, heads_per_group * head_size))
        log_sums.append(row_peak + jnp.log(denominator))
    return (jnp.concatenate(outputs, axis=1), log_sums)


def attention_backward(
    rotated_queries,
    rotated_keys,
    projected_values,
    allowed,
    log_sums,
    attended_grad,
    head_size,
    heads_per_group,
):
    count_of_rows = rotated_queries.shape[0]
    factor = head_size ** (-0.5)
    query_parts, key_parts, value_parts = ([], [], [])
    for member in range(len(log_sums)):
        queries = head_block(rotated_queries, member, heads_per_group * head_size).reshape(
            count_of_rows, heads_per_group, head_size
        )
        key_block = head_block(rotated_keys, member, head_size)
        value_block = head_block(projected_values, member, head_size)
        head_grads = head_block(attended_grad, member, heads_per_group * head_size).reshape(
            count_of_rows, heads_per_group, head_size
        )
        soft_probs = jnp.exp(
            masked_logits(queries, key_block, allowed, head_size) - log_sums[member]
        )
        prob_grad = jnp.einsum(
            "qcd,kd->cqk", head_grads, value_block, preferred_element_type=jnp.float32
        )
        logit_grad = (
            soft_probs * (prob_grad - jnp.sum(soft_probs * prob_grad, axis=-1, keepdims=True))
        ).astype(jnp.bfloat16)
        query_part = (
            jnp.einsum("cqk,kd->qcd", logit_grad, key_block, preferred_element_type=jnp.float32)
            * factor
        )
        query_parts.append(query_part.reshape(count_of_rows, heads_per_group * head_size))
        key_parts.append(
            jnp.einsum("cqk,qcd->kd", logit_grad, queries, preferred_element_type=jnp.float32)
            * factor
        )
        value_parts.append(
            jnp.einsum(
                "cqk,qcd->kd",
                soft_probs.astype(jnp.bfloat16),
                head_grads,
                preferred_element_type=jnp.float32,
            )
        )
    return (
        jnp.concatenate(query_parts, axis=1),
        jnp.concatenate(key_parts, axis=1),
        jnp.concatenate(value_parts, axis=1),
    )


def feed_forward(rows_in, gate_matrix, up_matrix):
    gate_value = jnp.dot(rows_in, gate_matrix, preferred_element_type=jnp.float32)
    up_value = jnp.dot(rows_in, up_matrix, preferred_element_type=jnp.float32)
    sigmoid_gate = jax.nn.sigmoid(gate_value)
    hidden = (gate_value * sigmoid_gate * up_value).astype(jnp.bfloat16)
    return (gate_value, up_value, sigmoid_gate, hidden)


def feed_backward(hidden_grad, gate_value, up_value, sigmoid_gate):
    gate_part = (
        hidden_grad * up_value * sigmoid_gate * (1.0 + gate_value * (1.0 - sigmoid_gate))
    ).astype(jnp.bfloat16)
    up_part = (hidden_grad * gate_value * sigmoid_gate).astype(jnp.bfloat16)
    return (gate_part, up_part)


def reduce_grads(partials, gain_parts):
    wide_done = (
        lax.psum_scatter(
            partials[0].astype(jnp.bfloat16), "wide", scatter_dimension=0, tiled=True
        ).astype(jnp.float32),
        lax.psum_scatter(
            partials[1].astype(jnp.bfloat16), "wide", scatter_dimension=0, tiled=True
        ).astype(jnp.float32),
        lax.psum_scatter(
            partials[2].astype(jnp.bfloat16), "wide", scatter_dimension=0, tiled=True
        ).astype(jnp.float32),
        lax.psum_scatter(
            partials[3].astype(jnp.bfloat16), "wide", scatter_dimension=0, tiled=True
        ).astype(jnp.float32),
        lax.psum_scatter(
            partials[4].astype(jnp.bfloat16), "wide", scatter_dimension=1, tiled=True
        ).astype(jnp.float32),
        lax.psum_scatter(
            partials[5].astype(jnp.bfloat16), "wide", scatter_dimension=1, tiled=True
        ).astype(jnp.float32),
        lax.psum_scatter(
            partials[6].astype(jnp.bfloat16), "wide", scatter_dimension=0, tiled=True
        ).astype(jnp.float32),
    )
    shards = (
        lax.psum_scatter(
            wide_done[0].astype(jnp.bfloat16), "narrow", scatter_dimension=1, tiled=True
        ).astype(jnp.float32),
        lax.psum_scatter(
            wide_done[1].astype(jnp.bfloat16), "narrow", scatter_dimension=1, tiled=True
        ).astype(jnp.float32),
        lax.psum_scatter(
            wide_done[2].astype(jnp.bfloat16), "narrow", scatter_dimension=1, tiled=True
        ).astype(jnp.float32),
        lax.psum_scatter(
            wide_done[3].astype(jnp.bfloat16), "narrow", scatter_dimension=1, tiled=True
        ).astype(jnp.float32),
        lax.psum_scatter(
            wide_done[4].astype(jnp.bfloat16), "narrow", scatter_dimension=0, tiled=True
        ).astype(jnp.float32),
        lax.psum_scatter(
            wide_done[5].astype(jnp.bfloat16), "narrow", scatter_dimension=0, tiled=True
        ).astype(jnp.float32),
        lax.psum_scatter(
            wide_done[6].astype(jnp.bfloat16), "narrow", scatter_dimension=1, tiled=True
        ).astype(jnp.float32),
    )
    gain_sums = lax.psum(gain_parts, ("wide", "narrow"))
    return (shards, gain_sums)


def body(
    tokens,
    lengths,
    cotangent,
    query_weight,
    key_matrix,
    value_matrix,
    output_weight,
    gate_weight,
    up_weight,
    down_weight,
    attention_gain,
    feedforward_gain,
):
    head_size = HEAD_WIDTH
    heads_per_group = QUERY_HEADS // KEY_VALUE_HEADS
    count_of_rows = tokens.shape[1]
    mixed_list = []
    grad_list = []
    collected = None
    for micro_index in range(tokens.shape[0]):
        columns = (
            lax.all_gather(query_weight, "narrow", axis=1, tiled=True),
            lax.all_gather(key_matrix, "narrow", axis=1, tiled=True),
            lax.all_gather(value_matrix, "narrow", axis=1, tiled=True),
            lax.all_gather(output_weight, "narrow", axis=1, tiled=True),
            lax.all_gather(gate_weight, "narrow", axis=0, tiled=True),
            lax.all_gather(up_weight, "narrow", axis=0, tiled=True),
            lax.all_gather(down_weight, "narrow", axis=1, tiled=True),
            lax.all_gather(attention_gain, "narrow", axis=0, tiled=True),
            lax.all_gather(feedforward_gain, "narrow", axis=0, tiled=True),
        )
        full_weights = (
            lax.all_gather(columns[0], "wide", axis=0, tiled=True),
            lax.all_gather(columns[1], "wide", axis=0, tiled=True),
            lax.all_gather(columns[2], "wide", axis=0, tiled=True),
            lax.all_gather(columns[3], "wide", axis=0, tiled=True),
            lax.all_gather(columns[4], "wide", axis=1, tiled=True),
            lax.all_gather(columns[5], "wide", axis=1, tiled=True),
            lax.all_gather(columns[6], "wide", axis=0, tiled=True),
        )
        query_full, key_full, value_full, output_full, gate_matrix, up_matrix, down_matrix = (
            full_weights
        )
        gain_first = columns[7].astype(jnp.float32)
        gain_second = columns[8].astype(jnp.float32)
        token_rows = tokens[micro_index].astype(jnp.float32)
        segment, position = segments_of(lengths[micro_index, 0], count_of_rows)
        valid_rows = (segment < lengths.shape[2]).astype(jnp.float32)[:, None]
        row_order = jnp.arange(count_of_rows, dtype=jnp.int32)
        allowed = (segment[:, None] == segment[None, :]) & (
            row_order[None, :] <= row_order[:, None]
        )
        cosine_table, sine_table = rotation_tables(position, head_size)
        attention_scale = rms_scale(token_rows)
        attention_in = (token_rows * attention_scale * gain_first).astype(jnp.bfloat16)
        query_value = jnp.dot(attention_in, query_full, preferred_element_type=jnp.float32)
        key_value = jnp.dot(attention_in, key_full, preferred_element_type=jnp.float32)
        projected_values = jnp.dot(
            attention_in, value_full, preferred_element_type=jnp.float32
        ).astype(jnp.bfloat16)
        rotated_queries = rotate(query_value, cosine_table, sine_table, head_size, False).astype(
            jnp.bfloat16
        )
        rotated_keys = rotate(key_value, cosine_table, sine_table, head_size, False).astype(
            jnp.bfloat16
        )
        attended, log_sums = attention_forward(
            rotated_queries, rotated_keys, projected_values, allowed, head_size, heads_per_group
        )
        attended_low = attended.astype(jnp.bfloat16)
        residual = token_rows + jnp.dot(
            attended_low, output_full, preferred_element_type=jnp.float32
        )
        feed_scale = rms_scale(residual)
        feed_in = (residual * feed_scale * gain_second).astype(jnp.bfloat16)
        out_grad = cotangent[micro_index].astype(jnp.float32) * valid_rows
        branch_grad = out_grad.astype(jnp.bfloat16)
        gate_value, up_value, sigmoid_gate, hidden = feed_forward(feed_in, gate_matrix, up_matrix)
        branch = jnp.dot(hidden, down_matrix, preferred_element_type=jnp.float32)
        hidden_grad = jnp.einsum(
            "rd,fd->rf", branch_grad, down_matrix, preferred_element_type=jnp.float32
        )
        down_part = jnp.einsum("rf,rd->fd", hidden, branch_grad, preferred_element_type=jnp.float32)
        gate_part, up_part = feed_backward(hidden_grad, gate_value, up_value, sigmoid_gate)
        feed_in_grad = jnp.einsum(
            "rf,df->rd", gate_part, gate_matrix, preferred_element_type=jnp.float32
        ) + jnp.einsum("rf,df->rd", up_part, up_matrix, preferred_element_type=jnp.float32)
        gate_wgrad = jnp.einsum("rd,rf->df", feed_in, gate_part, preferred_element_type=jnp.float32)
        up_wgrad = jnp.einsum("rd,rf->df", feed_in, up_part, preferred_element_type=jnp.float32)
        mixed_list.append((valid_rows * (residual + branch)).astype(jnp.bfloat16))
        residual_extra, feed_gain_part = rms_back(residual, feed_scale, gain_second, feed_in_grad)
        residual_grad = out_grad + residual_extra
        attention_branch_grad = residual_grad.astype(jnp.bfloat16)
        attended_grad = jnp.einsum(
            "rd,ed->re", attention_branch_grad, output_full, preferred_element_type=jnp.float32
        ).astype(jnp.bfloat16)
        output_wgrad = jnp.einsum(
            "re,rd->ed", attended_low, attention_branch_grad, preferred_element_type=jnp.float32
        )
        query_rot_grad, key_rot_grad, value_part = attention_backward(
            rotated_queries,
            rotated_keys,
            projected_values,
            allowed,
            log_sums,
            attended_grad,
            head_size,
            heads_per_group,
        )
        query_part = rotate(query_rot_grad, cosine_table, sine_table, head_size, True).astype(
            jnp.bfloat16
        )
        key_part = rotate(key_rot_grad, cosine_table, sine_table, head_size, True).astype(
            jnp.bfloat16
        )
        value_low = value_part.astype(jnp.bfloat16)
        attention_in_grad = jnp.einsum(
            "re,de->rd", query_part, query_full, preferred_element_type=jnp.float32
        )
        attention_in_grad = attention_in_grad + jnp.einsum(
            "re,de->rd", key_part, key_full, preferred_element_type=jnp.float32
        )
        attention_in_grad = attention_in_grad + jnp.einsum(
            "re,de->rd", value_low, value_full, preferred_element_type=jnp.float32
        )
        query_wgrad = jnp.einsum(
            "rd,re->de", attention_in, query_part, preferred_element_type=jnp.float32
        )
        key_wgrad = jnp.einsum(
            "rd,re->de", attention_in, key_part, preferred_element_type=jnp.float32
        )
        value_wgrad = jnp.einsum(
            "rd,re->de", attention_in, value_low, preferred_element_type=jnp.float32
        )
        token_extra, attention_gain_part = rms_back(
            token_rows, attention_scale, gain_first, attention_in_grad
        )
        grad_list.append((residual_grad + token_extra).astype(jnp.bfloat16))
        partials = (
            query_wgrad,
            key_wgrad,
            value_wgrad,
            output_wgrad,
            gate_wgrad,
            up_wgrad,
            down_part,
        )
        gain_parts = jnp.stack([attention_gain_part, feed_gain_part])
        reduced = reduce_grads(partials, gain_parts)
        collected = reduced if collected is None else jax.tree.map(jnp.add, collected, reduced)
    shards, gain_sums = collected
    shard_width = gain_sums.shape[1] // lax.axis_size("narrow")
    gain_start = lax.axis_index("narrow") * shard_width
    gain_shard = lax.dynamic_slice_in_dim(gain_sums, gain_start, shard_width, 1)
    return (
        jnp.stack(mixed_list),
        jnp.stack(grad_list),
        shards[0],
        shards[1],
        shards[2],
        shards[3],
        shards[4],
        shards[5],
        shards[6],
        gain_shard[0],
        gain_shard[1],
    )


def solution(mesh):
    in_specs = (
        P(None, ("wide", "narrow"), None),
        P(None, ("wide", "narrow"), None),
        P(None, ("wide", "narrow"), None),
        P("wide", "narrow"),
        P("wide", "narrow"),
        P("wide", "narrow"),
        P("wide", "narrow"),
        P("narrow", "wide"),
        P("narrow", "wide"),
        P("wide", "narrow"),
        P("narrow"),
        P("narrow"),
    )
    out_specs = (
        P(None, ("wide", "narrow"), None),
        P(None, ("wide", "narrow"), None),
        P("wide", "narrow"),
        P("wide", "narrow"),
        P("wide", "narrow"),
        P("wide", "narrow"),
        P("narrow", "wide"),
        P("narrow", "wide"),
        P("wide", "narrow"),
        P("narrow"),
        P("narrow"),
    )
    return jax.shard_map(body, mesh=mesh, in_specs=in_specs, out_specs=out_specs, check_vma=False)
```

profile of v0, /device:TPU:0, one launch (start us, length us, event | category | flops | bytes accessed | tf_op | source)
XLA Modules:
  0.0 1844.2 jit_solution(6511810569974380361)
XLA Ops:
  78.1 33.5 %all-gather = bf16[8,120,320]{1,2,0:T(8,128)(2,1)S(1)} all-gather(bf16[1,120,320]{1,2,0:T(8,128)(2,1)S(1)} %bitcast.844), channel_id=1, replica_groups=mesh['wide'=8,'narrow'=4] {'wide'}, dimensions={0}, use_global_device_ids=true | all-gather | bytes 691200 | tf_op jit(solution)/shard_map/all_gather | solution.py:261
  115.1 33.3 %all-gather.1 = bf16[8,120,320]{1,2,0:T(8,128)(2,1)S(1)} all-gather(bf16[1,120,320]{1,2,0:T(8,128)(2,1)S(1)} %bitcast.843), channel_id=1, replica_groups=mesh['wide'=8,'narrow'=4] {'wide'}, dimensions={0}, use_global_device_ids=true | all-gather | bytes 691200 | tf_op jit(solution)/shard_map/all_gather | solution.py:260
  198.2 12.2 all-gather.17.cloned.1.call-done
  217.3 79.6 %all-gather.15.cloned.1.call-done = bf16[960,2560]{0,1:T(8,128)(2,1)} async-done(((bf16[960,320]{0,1:T(8,128)(2,1)}), bf16[960,2560]{0,1:T(8,128)(2,1)}) %all-gather.15.cloned.1.call-update) | async-done | bytes 4915216 | tf_op jit(solution)/shard_map/all_gather | solution.py:263
  303.9 79.6 %all-gather.19.cloned.1.call-done = bf16[2560,960]{1,0:T(8,128)(2,1)} async-done(((bf16[320,960]{1,0:T(8,128)(2,1)}), bf16[2560,960]{1,0:T(8,128)(2,1)}) %all-gather.19.cloned.1.call-update) | async-done | bytes 4915216 | tf_op jit(solution)/shard_map/all_gather | solution.py:265
  383.5 10.7 multiply_convert_fusion.2
  548.0 42.0 %all-reduce.10.cloned.1.call-done = (bf16[960,320]{0,1:T(8,128)(2,1)}, bf16[960,320]{0,1:T(8,128)(2,1)}, bf16[960,320]{0,1:T(8,128)(2,1)}, bf16[960,320]{0,1:T(8,128)(2,1)}) async-done(((bf16[960,320]{0,1:T(8,128)(2,1)}, bf16[960,320]{0,1:T(8,128)(2,1)}, bf16[960,320]{0,1:T(8,128)(2,1)}, bf16[960,320]{0,1:T(8,128)(2,1)}), (bf16[960,320]{0,1:T(8,128)(2,1)}, bf16[960,320]{0,1:T(8,128)(2,1)}, ...) | async-done | bytes 2457616
  596.9 62.5 %reduce-scatter.61.cloned.1.call-done = bf16[120,960]{1,0:T(8,128)(2,1)} async-done(((bf16[960,960]{1,0:T(8,128)(2,1)}), bf16[120,960]{1,0:T(8,128)(2,1)}) %reduce-scatter.61.cloned.1.call-update) | async-done | bytes 230416 | tf_op jit(solution)/shard_map/reduce_scatter | solution.py:186
  661.3 67.8 %reduce-scatter.63.cloned.1.call-done = bf16[120,960]{1,0:T(8,128)(2,1)} async-done(((bf16[960,960]{1,0:T(8,128)(2,1)}), bf16[120,960]{1,0:T(8,128)(2,1)}) %reduce-scatter.63.cloned.1.call-update) | async-done | bytes 230416 | tf_op jit(solution)/shard_map/reduce_scatter | solution.py:186
  730.9 67.4 %reduce-scatter.51.cloned.1.call-done = bf16[120,960]{1,0:T(8,128)(2,1)} async-done(((bf16[960,960]{1,0:T(8,128)(2,1)}), bf16[120,960]{1,0:T(8,128)(2,1)}) %reduce-scatter.51.cloned.1.call-update) | async-done | bytes 230416 | tf_op jit(solution)/shard_map/reduce_scatter | solution.py:177
  800.4 67.3 %reduce-scatter.49.cloned.1.call-done = bf16[120,960]{1,0:T(8,128)(2,1)} async-done(((bf16[960,960]{1,0:T(8,128)(2,1)}), bf16[120,960]{1,0:T(8,128)(2,1)}) %reduce-scatter.49.cloned.1.call-update) | async-done | bytes 230416 | tf_op jit(solution)/shard_map/reduce_scatter | solution.py:177
  869.6 103.3 %reduce-scatter.73.cloned.1.call-done = bf16[320,960]{1,0:T(8,128)(2,1)} async-done(((bf16[2560,960]{1,0:T(8,128)(2,1)}), bf16[320,960]{1,0:T(8,128)(2,1)}) %reduce-scatter.73.cloned.1.call-update) | async-done | bytes 614416 | tf_op jit(solution)/shard_map/reduce_scatter | solution.py:195
  975.3 103.6 %reduce-scatter.75.cloned.1.call-done = bf16[320,960]{1,0:T(8,128)(2,1)} async-done(((bf16[2560,960]{1,0:T(8,128)(2,1)}), bf16[320,960]{1,0:T(8,128)(2,1)}) %reduce-scatter.75.cloned.1.call-update) | async-done | bytes 614416 | tf_op jit(solution)/shard_map/reduce_scatter | solution.py:195
  1088.4 96.5 %reduce-scatter.69.cloned.1.call-done = bf16[960,320]{0,1:T(8,128)(2,1)} async-done(((bf16[960,2560]{0,1:T(8,128)(2,1)}), bf16[960,320]{0,1:T(8,128)(2,1)}) %reduce-scatter.69.cloned.1.call-update) | async-done | bytes 614416 | tf_op jit(solution)/shard_map/reduce_scatter | solution.py:192
  1194.7 42.9 %psum.16 = f32[2,960]{1,0:T(2,128)S(1)} all-reduce(f32[2,960]{1,0:T(2,128)S(1)} %maximum_add_fusion), channel_id=1, replica_groups=mesh['wide'=8,'narrow'=4] {'wide','narrow'}, use_global_device_ids=true, to_apply=%region_74.75 | all-reduce | flops 1920 | bytes 15360 | tf_op jit(solution)/shard_map/psum | solution.py:222
  1237.6 54.1 %reduce-scatter.65.cloned.1.call-done = bf16[960,320]{0,1:T(8,128)(2,1)} async-done(((bf16[960,2560]{0,1:T(8,128)(2,1)}), bf16[960,320]{0,1:T(8,128)(2,1)}) %reduce-scatter.65.cloned.1.call-update) | async-done | bytes 614416 | tf_op jit(solution)/shard_map/reduce_scatter | solution.py:189
  1307.9 89.6 %reduce-scatter.71.cloned.1.call-done = bf16[960,320]{0,1:T(8,128)(2,1)} async-done(((bf16[960,2560]{0,1:T(8,128)(2,1)}), bf16[960,320]{0,1:T(8,128)(2,1)}) %reduce-scatter.71.cloned.1.call-update) | async-done | bytes 614416 | tf_op jit(solution)/shard_map/reduce_scatter | solution.py:192
  1406.8 96.5 %reduce-scatter.67.cloned.1.call-done = bf16[960,320]{0,1:T(8,128)(2,1)} async-done(((bf16[960,2560]{0,1:T(8,128)(2,1)}), bf16[960,320]{0,1:T(8,128)(2,1)}) %reduce-scatter.67.cloned.1.call-update) | async-done | bytes 614416 | tf_op jit(solution)/shard_map/reduce_scatter | solution.py:189
  1505.5 19.9 %reduce-scatter.55.cloned.1.call-done = bf16[120,80]{0,1:T(8,128)(2,1)} async-done(((bf16[120,320]{0,1:T(8,128)(2,1)}), bf16[120,80]{0,1:T(8,128)(2,1)}) %reduce-scatter.55.cloned.1.call-update) | async-done | bytes 19216 | tf_op jit(solution)/shard_map/reduce_scatter | solution.py:203
  1525.4 22.4 %reduce-scatter.53.cloned.1.call-done = bf16[120,80]{0,1:T(8,128)(2,1)} async-done(((bf16[120,320]{0,1:T(8,128)(2,1)}), bf16[120,80]{0,1:T(8,128)(2,1)}) %reduce-scatter.53.cloned.1.call-update) | async-done | bytes 19216 | tf_op jit(solution)/shard_map/reduce_scatter | solution.py:203
  1549.2 20.6 %reduce-scatter.57.cloned.1.call-done = bf16[120,80]{0,1:T(8,128)(2,1)} async-done(((bf16[120,320]{0,1:T(8,128)(2,1)}), bf16[120,80]{0,1:T(8,128)(2,1)}) %reduce-scatter.57.cloned.1.call-update) | async-done | bytes 19216 | tf_op jit(solution)/shard_map/reduce_scatter | solution.py:206
  1569.8 21.8 %reduce-scatter.59.cloned.1.call-done = bf16[120,80]{0,1:T(8,128)(2,1)} async-done(((bf16[120,320]{0,1:T(8,128)(2,1)}), bf16[120,80]{0,1:T(8,128)(2,1)}) %reduce-scatter.59.cloned.1.call-update) | async-done | bytes 19216 | tf_op jit(solution)/shard_map/reduce_scatter | solution.py:206
  1592.9 21.1 %reduce-scatter.81.cloned.1.call-done = bf16[240,120]{1,0:T(8,128)(2,1)} async-done(((bf16[960,120]{1,0:T(8,128)(2,1)}), bf16[240,120]{1,0:T(8,128)(2,1)}) %reduce-scatter.81.cloned.1.call-update) | async-done | bytes 57616
  1614.9 21.7 %reduce-scatter.83.cloned.1.call-done = bf16[240,120]{1,0:T(8,128)(2,1)} async-done(((bf16[960,120]{1,0:T(8,128)(2,1)}), bf16[240,120]{1,0:T(8,128)(2,1)}) %reduce-scatter.83.cloned.1.call-update) | async-done | bytes 57616
  1637.5 22.1 %reduce-scatter.79.cloned.1.call-done = bf16[240,120]{1,0:T(8,128)(2,1)} async-done(((bf16[960,120]{1,0:T(8,128)(2,1)}), bf16[240,120]{1,0:T(8,128)(2,1)}) %reduce-scatter.79.cloned.1.call-update) | async-done | bytes 57616
  1660.5 21.5 %reduce-scatter.77.cloned.1.call-done = bf16[240,120]{1,0:T(8,128)(2,1)} async-done(((bf16[960,120]{1,0:T(8,128)(2,1)}), bf16[240,120]{1,0:T(8,128)(2,1)}) %reduce-scatter.77.cloned.1.call-update) | async-done | bytes 57616
  1684.3 23.3 %reduce-scatter.93.cloned.1.call-done = bf16[240,320]{1,0:T(8,128)(2,1)} async-done(((bf16[960,320]{1,0:T(8,128)(2,1)}), bf16[240,320]{1,0:T(8,128)(2,1)}) %reduce-scatter.93.cloned.1.call-update) | async-done | bytes 153616
  1708.6 24.5 %reduce-scatter.95.cloned.1.call-done = bf16[240,320]{1,0:T(8,128)(2,1)} async-done(((bf16[960,320]{1,0:T(8,128)(2,1)}), bf16[240,320]{1,0:T(8,128)(2,1)}) %reduce-scatter.95.cloned.1.call-update) | async-done | bytes 153616
  1734.2 24.3 %reduce-scatter.89.cloned.1.call-done = bf16[240,320]{1,0:T(8,128)(2,1)} async-done(((bf16[960,320]{1,0:T(8,128)(2,1)}), bf16[240,320]{1,0:T(8,128)(2,1)}) %reduce-scatter.89.cloned.1.call-update) | async-done | bytes 153616
  1759.6 24.7 %reduce-scatter.85.cloned.1.call-done = bf16[240,320]{1,0:T(8,128)(2,1)} async-done(((bf16[960,320]{1,0:T(8,128)(2,1)}), bf16[240,320]{1,0:T(8,128)(2,1)}) %reduce-scatter.85.cloned.1.call-update) | async-done | bytes 153616
  1785.3 24.5 %reduce-scatter.91.cloned.1.call-done = bf16[240,320]{1,0:T(8,128)(2,1)} async-done(((bf16[960,320]{1,0:T(8,128)(2,1)}), bf16[240,320]{1,0:T(8,128)(2,1)}) %reduce-scatter.91.cloned.1.call-update) | async-done | bytes 153616
  1812.3 23.0 %reduce-scatter.87.cloned.1.call-done = bf16[240,320]{1,0:T(8,128)(2,1)} async-done(((bf16[960,320]{1,0:T(8,128)(2,1)}), bf16[240,320]{1,0:T(8,128)(2,1)}) %reduce-scatter.87.cloned.1.call-update) | async-done | bytes 153616
  (714 shorter events, 367.7 us)
Async XLA Ops:
  7.2 148.1 %all-gather.11.cloned.1.call-start = ((), (), s32[]{:S(2)}) async-start(), calls=%async_computation.24 | async-start | bytes 2211840 | tf_op jit(solution)/shard_map/all_gather | solution.py:259
  16.2 167.8 %all-gather.13.cloned.1.call-start = ((), (), s32[]{:S(2)}) async-start(), calls=%async_computation.25 | async-start | bytes 2211840 | tf_op jit(solution)/shard_map/all_gather | solution.py:262
  23.8 186.6 %all-gather.17.cloned.1.call-start = ((), (), s32[]{:S(2)}) async-start(), calls=%async_computation.27 | async-start | bytes 5898240 | tf_op jit(solution)/shard_map/all_gather | solution.py:264
  33.8 263.1 %all-gather.15.cloned.1.call-start = ((), (), s32[]{:S(2)}) async-start(), calls=%async_computation.26 | async-start | bytes 5898240 | tf_op jit(solution)/shard_map/all_gather | solution.py:263
  43.8 339.7 %all-gather.19.cloned.1.call-start = ((), (), s32[]{:S(2)}) async-start(), calls=%async_computation.28 | async-start | bytes 5898240 | tf_op jit(solution)/shard_map/all_gather | solution.py:265
  53.9 536.1 %all-reduce.10.cloned.1.call-start = ((), (), s32[]{:S(2)}) async-start(), calls=%async_computation.53 | async-start | bytes 5242880
  67.1 92.2 %copy-start.124 = (f32[960]{0:T(1024)}, f32[960]{0:T(1024)S(1)}, u32[]{:S(2)}) copy-start(f32[960]{0:T(1024)S(1)} %convert_element_type.438) | copy-start | bytes 11524
  474.7 184.7 %reduce-scatter.61.cloned.1.call-start = ((), (), s32[]{:S(2)}) async-start(), calls=%async_computation.35 | async-start | bytes 2211840 | tf_op jit(solution)/shard_map/reduce_scatter | solution.py:186
  478.8 250.3 %reduce-scatter.63.cloned.1.call-start = ((), (), s32[]{:S(2)}) async-start(), calls=%async_computation.36 | async-start | bytes 2211840 | tf_op jit(solution)/shard_map/reduce_scatter | solution.py:186
  483.8 314.5 %reduce-scatter.51.cloned.1.call-start = ((), (), s32[]{:S(2)}) async-start(), calls=%async_computation.30 | async-start | bytes 2211840 | tf_op jit(solution)/shard_map/reduce_scatter | solution.py:177
  492.8 374.9 %reduce-scatter.49.cloned.1.call-start = ((), (), s32[]{:S(2)}) async-start(), calls=%async_computation.29 | async-start | bytes 2211840 | tf_op jit(solution)/shard_map/reduce_scatter | solution.py:177
  501.9 471.0 %reduce-scatter.73.cloned.1.call-start = ((), (), s32[]{:S(2)}) async-start(), calls=%async_computation.41 | async-start | bytes 5898240 | tf_op jit(solution)/shard_map/reduce_scatter | solution.py:195
  509.6 569.3 %reduce-scatter.75.cloned.1.call-start = ((), (), s32[]{:S(2)}) async-start(), calls=%async_computation.42 | async-start | bytes 5898240 | tf_op jit(solution)/shard_map/reduce_scatter | solution.py:195
  517.3 667.6 %reduce-scatter.69.cloned.1.call-start = ((), (), s32[]{:S(2)}) async-start(), calls=%async_computation.39 | async-start | bytes 5898240 | tf_op jit(solution)/shard_map/reduce_scatter | solution.py:192
  524.8 766.8 %reduce-scatter.65.cloned.1.call-start = ((), (), s32[]{:S(2)}) async-start(), calls=%async_computation.37 | async-start | bytes 5898240 | tf_op jit(solution)/shard_map/reduce_scatter | solution.py:189
  532.0 865.5 %reduce-scatter.71.cloned.1.call-start = ((), (), s32[]{:S(2)}) async-start(), calls=%async_computation.40 | async-start | bytes 5898240 | tf_op jit(solution)/shard_map/reduce_scatter | solution.py:192
  539.0 964.2 %reduce-scatter.67.cloned.1.call-start = ((), (), s32[]{:S(2)}) async-start(), calls=%async_computation.38 | async-start | bytes 5898240 | tf_op jit(solution)/shard_map/reduce_scatter | solution.py:189
  546.1 979.3 %reduce-scatter.55.cloned.1.call-start = ((), (), s32[]{:S(2)}) async-start(), calls=%async_computation.32 | async-start | bytes 102400 | tf_op jit(solution)/shard_map/reduce_scatter | solution.py:203
  591.7 956.1 %reduce-scatter.53.cloned.1.call-start = ((), (), s32[]{:S(2)}) async-start(), calls=%async_computation.31 | async-start | bytes 102400 | tf_op jit(solution)/shard_map/reduce_scatter | solution.py:203
  593.4 976.4 %reduce-scatter.57.cloned.1.call-start = ((), (), s32[]{:S(2)}) async-start(), calls=%async_computation.33 | async-start | bytes 102400 | tf_op jit(solution)/shard_map/reduce_scatter | solution.py:206
  595.1 996.4 %reduce-scatter.59.cloned.1.call-start = ((), (), s32[]{:S(2)}) async-start(), calls=%async_computation.34 | async-start | bytes 102400 | tf_op jit(solution)/shard_map/reduce_scatter | solution.py:206
  596.8 1017.1 %reduce-scatter.81.cloned.1.call-start = ((), (), s32[]{:S(2)}) async-start(), calls=%async_computation.45 | async-start | bytes 307200
  661.2 975.4 %reduce-scatter.83.cloned.1.call-start = ((), (), s32[]{:S(2)}) async-start(), calls=%async_computation.46 | async-start | bytes 307200
  730.9 928.7 %reduce-scatter.79.cloned.1.call-start = ((), (), s32[]{:S(2)}) async-start(), calls=%async_computation.44 | async-start | bytes 307200
  800.1 881.9 %reduce-scatter.77.cloned.1.call-start = ((), (), s32[]{:S(2)}) async-start(), calls=%async_computation.43 | async-start | bytes 307200
  869.5 838.1 %reduce-scatter.93.cloned.1.call-start = ((), (), s32[]{:S(2)}) async-start(), calls=%async_computation.51 | async-start | bytes 921600
  975.2 106.1 %copy-start.70 = (bf16[384,5,64]{0,2,1:T(8,128)(2,1)S(1)}, bf16[384,5,64]{0,2,1:T(8,128)(2,1)}, u32[]{:S(2)}) copy-start(bf16[384,5,64]{0,2,1:T(8,128)(2,1)} %copy-done.69) | copy-start | bytes 737284
  975.2 757.9 %reduce-scatter.95.cloned.1.call-start = ((), (), s32[]{:S(2)}) async-start(), calls=%async_computation.52 | async-start | bytes 921600
  1081.2 677.3 %reduce-scatter.89.cloned.1.call-start = ((), (), s32[]{:S(2)}) async-start(), calls=%async_computation.49 | async-start | bytes 921600
  1187.2 597.1 %reduce-scatter.85.cloned.1.call-start = ((), (), s32[]{:S(2)}) async-start(), calls=%async_computation.47 | async-start | bytes 921600
  1294.0 515.8 %reduce-scatter.91.cloned.1.call-start = ((), (), s32[]{:S(2)}) async-start(), calls=%async_computation.50 | async-start | bytes 921600
  1399.8 435.6 %reduce-scatter.87.cloned.1.call-start = ((), (), s32[]{:S(2)}) async-start(), calls=%async_computation.48 | async-start | bytes 921600
  (196 other events, 796.0 us)
Sparse Core Ops, SparseCore 0:
  16.3 48.8 all-gather.10
  68.0 53.6 all-gather.12
  123.9 86.5 all-gather.16
  212.5 84.4 all-gather.14
  299.0 84.4 all-gather.18
  474.8 115.1 all-reduce.9
  593.5 65.8 reduce-scatter.60
  663.3 65.7 reduce-scatter.62
  732.5 65.7 reduce-scatter.50
  802.0 65.6 reduce-scatter.48
  871.3 101.5 reduce-scatter.72
  976.4 102.4 reduce-scatter.74
  1082.5 102.3 reduce-scatter.68
  1188.3 103.3 reduce-scatter.64
  1295.1 102.3 reduce-scatter.70
  1400.9 102.3 reduce-scatter.66
  1506.1 19.2 reduce-scatter.54
  1528.3 19.4 reduce-scatter.52
  1550.2 19.4 reduce-scatter.56
  1572.0 19.4 reduce-scatter.58
  1594.0 19.9 reduce-scatter.80
  1616.6 19.9 reduce-scatter.82
  1639.6 19.9 reduce-scatter.78
  1662.1 19.9 reduce-scatter.76
  1684.6 22.9 reduce-scatter.92
  1710.2 22.9 reduce-scatter.94
  1735.6 22.9 reduce-scatter.88
  1761.2 22.9 reduce-scatter.84
  1786.8 22.9 reduce-scatter.90
  1812.3 22.9 reduce-scatter.86
where the time goes:
time: 1850 us; the launch traced here: 1840 us
  waiting for transfers between devices  1340 us (72%)
  matrix products  198 us (11%)
  blocking collectives  165 us (9%)
  local copies, waits for them, and re-layouts  87.5 us (5%)
  other arithmetic  35.6 us (2%)
  between operations  18.6 us (1%)
    unnamed x41, waiting for transfers between devices  273 us
    reduce_scatter x2, waiting for transfers between devices, reduce_grads(): lax.psum_scatter(partials[6].astype(jnp.bfloat16), 'wide', scatter_dimens...  207 us
    reduce_scatter x2, waiting for transfers between devices, reduce_grads(): lax.psum_scatter(partials[5].astype(jnp.bfloat16), 'wide', scatter_dimens...  186 us
    reduce_scatter x2, waiting for transfers between devices, reduce_grads(): lax.psum_scatter(partials[4].astype(jnp.bfloat16), 'wide', scatter_dimens...  151 us
    reduce_scatter x2, waiting for transfers between devices, reduce_grads(): lax.psum_scatter(partials[0].astype(jnp.bfloat16), 'wide', scatter_dimens...  135 us
    reduce_scatter x2, waiting for transfers between devices, reduce_grads(): lax.psum_scatter(partials[3].astype(jnp.bfloat16), 'wide', scatter_dimens...  130 us
    all_gather x1, waiting for transfers between devices, body(): lax.all_gather(columns[4], 'wide', axis=1, tiled=True)  79.6 us
    all_gather x1, waiting for transfers between devices, body(): lax.all_gather(columns[6], 'wide', axis=0, tiled=True)  79.6 us
  transfers between devices with their start and end apart: 30, of which 28 were waited for; matrix products, arithmetic and copies ran while one was open for 11% of the time, Pallas kernels for 0%

commit v1 on v0

v1 whole, which is shorter than its diff:
```python
import functools

import jax
import jax.numpy as jnp
from jax import lax
from jax.experimental import pallas as pl
from jax.experimental.pallas import tpu as pltpu
from jax.sharding import PartitionSpec as P

QUERY_HEADS = 15
KEY_VALUE_HEADS = 5
HEAD_WIDTH = 64


EPS = 1e-05
THETA = 10000.0


def segments_of(lengths_row, count_of_rows):
    ends = jnp.cumsum(lengths_row, dtype=jnp.int32)
    starts = ends - lengths_row
    places = jnp.arange(count_of_rows, dtype=jnp.int32)
    segment = jnp.sum((places[:, None] >= ends[None, :]).astype(jnp.int32), axis=1, dtype=jnp.int32)
    slot_ids = jnp.arange(lengths_row.shape[0], dtype=jnp.int32)
    opening = jnp.sum(
        jnp.where(segment[:, None] == slot_ids[None, :], starts[None, :], 0),
        axis=1,
        dtype=jnp.int32,
    )
    opening = jnp.where(segment == lengths_row.shape[0], ends[-1], opening)
    return (segment, places - opening)


def rotation_tables(position, head_size):
    half = head_size // 2
    freqs = THETA ** (-jnp.arange(half, dtype=jnp.float32) * 2.0 / head_size)
    angles = position.astype(jnp.float32)[:, None] * freqs[None, :]
    return (jnp.cos(angles)[:, None, :], jnp.sin(angles)[:, None, :])


def rotate(field, cosine_table, sine_table, head_size, inverse):
    count_of_rows = field.shape[0]
    pieces = field.reshape(count_of_rows, -1, head_size)
    half = head_size // 2
    left_half = pieces[..., :half]
    right_half = pieces[..., half:]
    sine_used = -sine_table if inverse else sine_table
    turned = jnp.concatenate(
        [
            left_half * cosine_table - right_half * sine_used,
            right_half * cosine_table + left_half * sine_used,
        ],
        axis=-1,
    )
    return turned.reshape(count_of_rows, -1)


def rms_scale(field):
    return lax.rsqrt(jnp.mean(field * field, axis=1, keepdims=True) + EPS)


def rms_back(field, scale, gain, upstream):
    normed = field * scale
    gain_grad = jnp.sum(upstream * normed, axis=0)
    normed_grad = upstream * gain
    field_grad = scale * (
        normed_grad - normed * jnp.mean(normed_grad * normed, axis=1, keepdims=True)
    )
    return (field_grad, gain_grad)


def head_block(matrix, member, width):
    return matrix[:, member * width : (member + 1) * width]


def masked_logits(queries, key_block, allowed, head_size):
    logits = jnp.einsum(
        "qcd,kd->cqk", queries, key_block, preferred_element_type=jnp.float32
    ) * head_size ** (-0.5)
    return jnp.where(allowed[None], logits, -1000000000.0)


def attention_forward(
    rotated_queries, rotated_keys, projected_values, allowed, head_size, heads_per_group
):
    count_of_rows = rotated_queries.shape[0]
    outputs = []
    log_sums = []
    for member in range(rotated_keys.shape[1] // head_size):
        queries = head_block(rotated_queries, member, heads_per_group * head_size).reshape(
            count_of_rows, heads_per_group, head_size
        )
        key_block = head_block(rotated_keys, member, head_size)
        value_block = head_block(projected_values, member, head_size)
        logits = masked_logits(queries, key_block, allowed, head_size)
        row_peak = jnp.max(logits, axis=-1, keepdims=True)
        shifted = jnp.exp(logits - row_peak)
        denominator = jnp.sum(shifted, axis=-1, keepdims=True)
        soft_probs = (shifted / denominator).astype(jnp.bfloat16)
        attended = jnp.einsum(
            "cqk,kd->qcd", soft_probs, value_block, preferred_element_type=jnp.float32
        )
        outputs.append(attended.reshape(count_of_rows, heads_per_group * head_size))
        log_sums.append(row_peak + jnp.log(denominator))
    return (jnp.concatenate(outputs, axis=1), log_sums)


def attention_backward(
    rotated_queries,
    rotated_keys,
    projected_values,
    allowed,
    log_sums,
    attended_grad,
    head_size,
    heads_per_group,
):
    count_of_rows = rotated_queries.shape[0]
    factor = head_size ** (-0.5)
    query_parts, key_parts, value_parts = ([], [], [])
    for member in range(len(log_sums)):
        queries = head_block(rotated_queries, member, heads_per_group * head_size).reshape(
            count_of_rows, heads_per_group, head_size
        )
        key_block = head_block(rotated_keys, member, head_size)
        value_block = head_block(projected_values, member, head_size)
        head_grads = head_block(attended_grad, member, heads_per_group * head_size).reshape(
            count_of_rows, heads_per_group, head_size
        )
        soft_probs = jnp.exp(
            masked_logits(queries, key_block, allowed, head_size) - log_sums[member]
        )
        prob_grad = jnp.einsum(
            "qcd,kd->cqk", head_grads, value_block, preferred_element_type=jnp.float32
        )
        logit_grad = (
            soft_probs * (prob_grad - jnp.sum(soft_probs * prob_grad, axis=-1, keepdims=True))
        ).astype(jnp.bfloat16)
        query_part = (
            jnp.einsum("cqk,kd->qcd", logit_grad, key_block, preferred_element_type=jnp.float32)
            * factor
        )
        query_parts.append(query_part.reshape(count_of_rows, heads_per_group * head_size))
        key_parts.append(
            jnp.einsum("cqk,qcd->kd", logit_grad, queries, preferred_element_type=jnp.float32)
            * factor
        )
        value_parts.append(
            jnp.einsum(
                "cqk,qcd->kd",
                soft_probs.astype(jnp.bfloat16),
                head_grads,
                preferred_element_type=jnp.float32,
            )
        )
    return (
        jnp.concatenate(query_parts, axis=1),
        jnp.concatenate(key_parts, axis=1),
        jnp.concatenate(value_parts, axis=1),
    )


F32=jnp.float32; BF=jnp.bfloat16
NT=(((1,),(1,)),((),()))
TN=(((0,),(0,)),((),()))
NN=(((1,),(0,)),((),()))
def dot(a,b,dn): return lax.dot_general(a,b,dn,preferred_element_type=F32)

def ffn_kernel(tile, bf_ref, gf_ref, own_ref, other_ref, own_grad, other_grad, mix_ref, gbf_ref, mix_acc, gbf_acc):
    step = pl.program_id(0)
    pair, wide, _, sub, lanes = own_ref.shape

    def weight(kind):
        parts = [
            ref[at, :, kind].reshape(tile, lanes) for ref in (own_ref, other_ref) for at in range(pair)
        ]
        return jnp.concatenate(parts, axis=1)

    gate, up, down = weight(0), weight(1), weight(2)
    rows_in = bf_ref[...]
    grad_in = gf_ref[...]
    gate_value = dot(rows_in, gate, NT)
    up_value = dot(rows_in, up, NT)
    hidden_grad = dot(grad_in, down, NT)
    sigmoid_gate = 1.0 / (1.0 + jnp.exp(-gate_value))
    silu = gate_value * sigmoid_gate
    hidden = (silu * up_value).astype(BF)
    gate_part = (hidden_grad * up_value * (sigmoid_gate * (1.0 + gate_value * (1.0 - sigmoid_gate)))).astype(BF)
    up_part = (hidden_grad * silu).astype(BF)
    mix = dot(hidden, down, NN)
    back = dot(gate_part, gate, NN) + dot(up_part, up, NN)

    @pl.when(step == 0)
    def _():
        mix_acc[...] = mix
        gbf_acc[...] = back

    @pl.when(step > 0)
    def _():
        mix_acc[...] += mix
        gbf_acc[...] += back

    for kind, (left, right) in enumerate(((gate_part, rows_in), (up_part, rows_in), (hidden, grad_in))):
        term = dot(left, right, TN).astype(BF)
        for index in range(2 * pair):
            ref = (own_grad, other_grad)[index // pair]
            ref[index % pair, :, kind] = term[:, index * lanes : (index + 1) * lanes].reshape(wide, sub, lanes)

    @pl.when(step == pl.num_programs(0) - 1)
    def _():
        mix_ref[...] = mix_acc[...]
        gbf_ref[...] = gbf_acc[...]


def ffn_call(rows_in, grad_in, own, other):
    pair, wide, _, units, lanes = own.shape
    rows, width = rows_in.shape
    tile = 256
    sub = tile // wide
    steps = units // sub
    weight_spec = pl.BlockSpec((pair, wide, 3, sub, lanes), lambda t: (0, 0, 0, t, 0))
    whole = pl.BlockSpec((rows, width), lambda t: (0, 0))
    own_terms, other_terms, mix, back = pl.pallas_call(
        functools.partial(ffn_kernel, tile),
        grid=(steps,),
        in_specs=[whole, whole, weight_spec, weight_spec],
        out_specs=[weight_spec, weight_spec, whole, whole],
        out_shape=[jax.ShapeDtypeStruct(own.shape, BF)] * 2 + [jax.ShapeDtypeStruct((rows, width), F32)] * 2,
        scratch_shapes=[pltpu.VMEM((rows, width), F32)] * 2,
        compiler_params=pltpu.CompilerParams(vmem_limit_bytes=56 * 1024 * 1024),
        cost_estimate=pl.CostEstimate(
            flops=18 * rows * width * units * wide,
            bytes_accessed=rows * width * 12 + 4 * own.size * 2,
            transcendentals=rows * units * wide,
        ),
        name="feed_forward",
    )(rows_in, grad_in, own, other)
    return mix, back, own_terms, other_terms


AXES = ("wide", "narrow")


class Grid:
    def __init__(self):
        self.wide = lax.axis_size("wide")
        self.narrow = lax.axis_size("narrow")
        self.outer = 4
        self.inner = self.wide // 4
        self.pair = self.narrow // 2
        self.size = {"outer": 4, "inner": self.inner, "pair": self.pair, "core": 2}
        self.stride = {"outer": self.inner * self.narrow, "inner": self.narrow, "pair": 2, "core": 1}
        linear = lax.axis_index("wide") * self.narrow + lax.axis_index("narrow")
        self.at = {name: (linear // self.stride[name]) % self.size[name] for name in self.size}

    def shift(self, value, name):
        size, stride = self.size[name], self.stride[name]
        pairs = []
        for source in range(self.wide * self.narrow):
            digit = (source // stride) % size
            pairs.append((source, source + ((digit + 1) % size - digit) * stride))
        return lax.ppermute(value, AXES, pairs)

    def gather(self, block, name):
        blocks = [block]
        for _ in range(self.size[name] - 1):
            blocks.append(self.shift(blocks[-1], name))
        return blocks

    def in_order(self, blocks, name):
        size = self.size[name]
        doubled = jnp.stack(blocks[::-1] + blocks[:0:-1])
        return lax.dynamic_slice_in_dim(doubled, size - 1 - self.at[name], size, 0)

    def scatter(self, pick, name):
        size = self.size[name]
        total = pick(1)
        for step in range(1, size):
            total = self.shift(total, name) + pick((step + 1) % size)
        return total

    def behind(self, name, steps):
        return (self.at[name] + (self.size[name] - steps)) % self.size[name]


def chosen(array, index):
    return lax.dynamic_index_in_dim(array, index, 0, keepdims=False)


def gather_chunk(grid, shard, cut):
    ring = grid.gather(shard, "outer")
    first = jnp.stack([part[:, :cut] for part in ring])
    second = jnp.stack([part[:, cut:] for part in ring])
    first_wide = jnp.concatenate(grid.gather(first, "inner"))
    second_pair = jnp.stack(grid.gather(second, "pair"))
    first_all = jnp.stack(grid.gather(first_wide, "pair"))
    second_all = jnp.concatenate(grid.gather(second_pair, "inner"), axis=1)
    own = jnp.concatenate([first_all, second_all], axis=3)
    return own, grid.shift(own, "core")


def scatter_chunk(grid, own, other, cut):
    outer = grid.outer
    both = grid.shift(other, "core") + own
    first = grid.scatter(lambda r: both[r, :, :, :cut], "pair")
    first = grid.scatter(lambda r: first[r * outer : (r + 1) * outer], "inner")
    second_wide = grid.scatter(lambda r: both[:, r * outer : (r + 1) * outer, :, cut:], "inner")
    second = grid.scatter(lambda r: second_wide[r], "pair")
    merged = jnp.concatenate([first, second], axis=2)
    return grid.scatter(lambda r: merged[r], "outer")


def gather_attention(grid, shard):
    cut = shard.shape[0] // 2
    ring = grid.in_order(grid.gather(shard, "outer"), "outer")
    first = grid.in_order(grid.gather(ring[:, :cut], "inner"), "inner")
    second = grid.in_order(grid.gather(ring[:, cut:], "pair"), "pair")
    first = grid.in_order(grid.gather(first, "pair"), "pair")
    second = grid.in_order(grid.gather(second, "inner"), "inner")
    own = jnp.concatenate([first, jnp.swapaxes(second, 0, 1)], axis=3)
    return grid.in_order(grid.gather(own, "core"), "core")


def scatter_attention(grid, terms):
    cut = terms.shape[4] // 2
    both = grid.scatter(lambda r: chosen(terms, grid.behind("core", r)), "core")
    first_terms = both[:, :, :, :cut]
    first_inner = grid.scatter(lambda r: chosen(first_terms, grid.behind("pair", r)), "pair")
    first = grid.scatter(lambda r: chosen(first_inner, grid.behind("inner", r)), "inner")
    second_terms = jnp.swapaxes(both[:, :, :, cut:], 0, 1)
    second_pair = grid.scatter(lambda r: chosen(second_terms, grid.behind("inner", r)), "inner")
    second = grid.scatter(lambda r: chosen(second_pair, grid.behind("pair", r)), "pair")
    merged = jnp.concatenate([first, second], axis=1)
    return grid.scatter(lambda r: chosen(merged, grid.behind("outer", r)), "outer")


def rounded_up(count, step):
    return -(-count // step) * step


def body(
    tokens,
    lengths,
    cotangent,
    query_weight,
    key_matrix,
    value_matrix,
    output_weight,
    gate_weight,
    up_weight,
    down_weight,
    attention_gain,
    feedforward_gain,
):
    grid = Grid()
    head_size = HEAD_WIDTH
    heads_per_group = QUERY_HEADS // KEY_VALUE_HEADS
    batches, bucket_rows, width = tokens.shape
    rows = batches * bucket_rows
    wide, narrow, pair = grid.wide, grid.narrow, grid.pair
    d_w, d_n = query_weight.shape
    kv_n = key_matrix.shape[1]
    f_w = down_weight.shape[0]
    d_pad = rounded_up(d_n, 128)
    a_rows = rounded_up(d_w + 2, 32)

    packed = jnp.concatenate([query_weight, output_weight, key_matrix, value_matrix], axis=1)
    lanes = packed.shape[1]
    gains = jnp.concatenate([attention_gain, feedforward_gain, jnp.zeros((2 * kv_n,), BF)])
    a_shard = jnp.concatenate([packed, jnp.zeros((a_rows - d_w, lanes), BF).at[0].set(gains)], axis=0)
    f_shard = jnp.pad(
        jnp.stack([gate_weight.T, up_weight.T, down_weight]), ((0, 0), (0, 0), (0, d_pad - d_n))
    )
    sub = 256 // wide
    half = f_w // 2
    cut = (half // sub + 1) // 2 * sub

    a_all = gather_attention(grid, a_shard)
    chunks = [gather_chunk(grid, f_shard[:, i * half : (i + 1) * half], cut) for i in range(2)]

    def natural(lo, count):
        block = a_all[:, :, :, :, :d_w, lo : lo + count]
        return block.transpose(3, 2, 4, 1, 0, 5).reshape(wide * d_w, narrow * count)

    query_full = natural(0, d_n)
    key_full = natural(2 * d_n, kv_n)
    value_full = natural(2 * d_n + kv_n, kv_n)
    order = [
        (grid.behind("core", dc), grid.behind("pair", dy)) for dc in range(2) for dy in range(pair)
    ]
    by_narrow = a_all.reshape(2 * pair, *a_all.shape[2:])
    relative = [c_at * pair + y_at for c_at, y_at in order]

    def padded(block):
        return jnp.pad(block, ((0, 0), (0, d_pad - d_n)))

    output_parts = []
    gain_first_parts = []
    gain_second_parts = []
    for index in range(narrow):
        gain_first_parts.append(by_narrow[(index % 2) * pair + index // 2, 0, 0, d_w, :d_n])
    for index in relative:
        block = chosen(by_narrow, index)
        output_parts.append(
            padded(
                block[:, :, :d_w, d_n : 2 * d_n].transpose(1, 0, 2, 3).reshape(wide * d_w, d_n)
            )
        )
        gain_second_parts.append(jnp.pad(block[0, 0, d_w, d_n : 2 * d_n], (0, d_pad - d_n)))
    output_full = jnp.concatenate(output_parts, axis=1)
    gain_first = jnp.concatenate(gain_first_parts).astype(F32)
    gain_second = jnp.concatenate(gain_second_parts).astype(F32)

    def to_relative(field):
        stacked = jnp.stack([padded(field[:, i * d_n : (i + 1) * d_n]) for i in range(narrow)])
        return jnp.concatenate([chosen(stacked, y_at * 2 + c_at) for c_at, y_at in order], axis=1)

    def to_natural(field):
        stacked = jnp.stack([field[:, i * d_pad : i * d_pad + d_n] for i in range(narrow)])
        blocks = []
        for index in range(narrow):
            dc = (grid.at["core"] + index % 2) % 2
            dy = (grid.at["pair"] - index // 2 + pair) % pair
            blocks.append(chosen(stacked, dc * pair + dy))
        return jnp.concatenate(blocks, axis=1)

    token_low = tokens.reshape(rows, width)
    token_rows = token_low.astype(F32)
    token_relative = to_relative(token_low).astype(F32)
    tables = [segments_of(lengths[m, 0], bucket_rows) for m in range(batches)]
    row_order = jnp.arange(bucket_rows, dtype=jnp.int32)
    allowed = [
        (segment[:, None] == segment[None, :]) & (row_order[None, :] <= row_order[:, None])
        for segment, _ in tables
    ]
    valid_rows = jnp.concatenate(
        [(segment < lengths.shape[2]).astype(F32)[:, None] for segment, _ in tables]
    )
    cosine_table, sine_table = rotation_tables(
        jnp.concatenate([position for _, position in tables]), head_size
    )
    attention_scale = rms_scale(token_rows)
    attention_in = (token_rows * attention_scale * gain_first).astype(BF)
    query_value = jnp.dot(attention_in, query_full, preferred_element_type=F32)
    key_value = jnp.dot(attention_in, key_full, preferred_element_type=F32)
    projected_values = jnp.dot(attention_in, value_full, preferred_element_type=F32).astype(BF)
    rotated_queries = rotate(query_value, cosine_table, sine_table, head_size, False).astype(BF)
    rotated_keys = rotate(key_value, cosine_table, sine_table, head_size, False).astype(BF)

    def bucket(field, m):
        return field[m * bucket_rows : (m + 1) * bucket_rows]

    attended_parts = []
    log_sums = []
    for m in range(batches):
        attended, sums = attention_forward(
            bucket(rotated_queries, m),
            bucket(rotated_keys, m),
            bucket(projected_values, m),
            allowed[m],
            head_size,
            heads_per_group,
        )
        attended_parts.append(attended)
        log_sums.append(sums)
    attended_low = jnp.concatenate(attended_parts).astype(BF)

    def mean(field):
        return jnp.sum(field, axis=1, keepdims=True) / width

    residual = token_relative + jnp.dot(attended_low, output_full, preferred_element_type=F32)
    feed_scale = lax.rsqrt(mean(residual * residual) + EPS)
    feed_normed = residual * feed_scale
    feed_in = (feed_normed * gain_second).astype(BF)
    out_grad = to_relative(cotangent.reshape(rows, width)).astype(F32) * valid_rows
    branch_grad = out_grad.astype(BF)

    branch, feed_in_grad = 0.0, 0.0
    feed_shards = []
    for own, other in chunks:
        mix, grad_in, own_terms, other_terms = ffn_call(feed_in, branch_grad, own, other)
        branch = branch + mix
        feed_in_grad = feed_in_grad + grad_in
        feed_shards.append(scatter_chunk(grid, own_terms, other_terms, cut))
    mixed = to_natural((valid_rows * (residual + branch)).astype(BF))

    feed_gain_part = jnp.sum(feed_in_grad * feed_normed, axis=0)
    normed_grad = feed_in_grad * gain_second
    residual_grad = out_grad + feed_scale * (
        normed_grad - feed_normed * mean(normed_grad * feed_normed)
    )
    attention_branch_grad = residual_grad.astype(BF)
    attended_grad = dot(attention_branch_grad, output_full, NT).astype(BF)
    output_wgrad = dot(attended_low, attention_branch_grad, TN).astype(BF)
    backward = [
        attention_backward(
            bucket(rotated_queries, m),
            bucket(rotated_keys, m),
            bucket(projected_values, m),
            allowed[m],
            log_sums[m],
            bucket(attended_grad, m),
            head_size,
            heads_per_group,
        )
        for m in range(batches)
    ]
    query_rot_grad, key_rot_grad, value_part = [
        jnp.concatenate([parts[i] for parts in backward]) for i in range(3)
    ]
    query_part = rotate(query_rot_grad, cosine_table, sine_table, head_size, True).astype(BF)
    key_part = rotate(key_rot_grad, cosine_table, sine_table, head_size, True).astype(BF)
    value_low = value_part.astype(BF)
    attention_in_grad = (
        dot(query_part, query_full, NT)
        + dot(key_part, key_full, NT)
        + dot(value_low, value_full, NT)
    )
    query_wgrad = dot(attention_in, query_part, TN).astype(BF)
    key_wgrad = dot(attention_in, key_part, TN).astype(BF)
    value_wgrad = dot(attention_in, value_low, TN).astype(BF)
    token_extra, attention_gain_part = rms_back(
        token_rows, attention_scale, gain_first, attention_in_grad
    )
    tokens_grad = (to_natural(residual_grad) + token_extra).astype(BF)

    def blocked(field, count):
        return field.reshape(grid.outer, grid.inner, d_w, pair, 2, count).transpose(4, 3, 1, 0, 2, 5)

    stacked = jnp.stack([output_wgrad[:, i * d_pad : i * d_pad + d_n] for i in range(narrow)])
    output_natural = []
    for index in range(narrow):
        dc = (grid.at["core"] + index % 2) % 2
        dy = (grid.at["pair"] - index // 2 + pair) % pair
        output_natural.append(chosen(stacked, dc * pair + dy))
    terms = jnp.concatenate(
        [
            blocked(query_wgrad, d_n),
            blocked(jnp.concatenate(output_natural, axis=1), d_n),
            blocked(key_wgrad, kv_n),
            blocked(value_wgrad, kv_n),
        ],
        axis=5,
    )
    feed_gain_natural = to_natural(feed_gain_part[None])[0]
    gain_terms = jnp.concatenate(
        [
            attention_gain_part.reshape(pair, 2, d_n).transpose(1, 0, 2),
            feed_gain_natural.reshape(pair, 2, d_n).transpose(1, 0, 2),
            jnp.zeros((2, pair, 2 * kv_n), F32),
        ],
        axis=2,
    ).astype(BF)
    gain_terms = jnp.broadcast_to(
        gain_terms[:, :, None, None, None, :], (2, pair, grid.inner, grid.outer, 1, lanes)
    )
    spare = jnp.zeros((2, pair, grid.inner, grid.outer, a_rows - d_w - 1, lanes), BF)
    a_sum = scatter_attention(grid, jnp.concatenate([terms, gain_terms, spare], axis=4)).astype(F32)
    feed_sum = jnp.concatenate(feed_shards, axis=1).astype(F32)[:, :, :d_n]
    return (
        mixed.reshape(tokens.shape),
        tokens_grad.reshape(tokens.shape),
        a_sum[:d_w, :d_n],
        a_sum[:d_w, 2 * d_n : 2 * d_n + kv_n],
        a_sum[:d_w, 2 * d_n + kv_n :],
        a_sum[:d_w, d_n : 2 * d_n],
        feed_sum[0].T,
        feed_sum[1].T,
        feed_sum[2],
        a_sum[d_w, :d_n],
        a_sum[d_w, d_n : 2 * d_n],
    )


def solution(mesh):
    in_specs = (
        P(None, ("wide", "narrow"), None),
        P(None, ("wide", "narrow"), None),
        P(None, ("wide", "narrow"), None),
        P("wide", "narrow"),
        P("wide", "narrow"),
        P("wide", "narrow"),
        P("wide", "narrow"),
        P("narrow", "wide"),
        P("narrow", "wide"),
        P("wide", "narrow"),
        P("narrow"),
        P("narrow"),
    )
    out_specs = (
        P(None, ("wide", "narrow"), None),
        P(None, ("wide", "narrow"), None),
        P("wide", "narrow"),
        P("wide", "narrow"),
        P("wide", "narrow"),
        P("wide", "narrow"),
        P("narrow", "wide"),
        P("narrow", "wide"),
        P("wide", "narrow"),
        P("narrow"),
        P("narrow"),
    )
    return jax.shard_map(body, mesh=mesh, in_specs=in_specs, out_specs=out_specs, check_vma=False)
```

time: 1850 us -> 628 us (0.34)
  waiting for transfers between devices: 1340 us -> 171 us
  blocking collectives: 165 us -> 0 us
  matrix products: 198 us -> 61.1 us
  other arithmetic: 35.6 us -> 120 us
  local copies, waits for them, and re-layouts: 87.5 us -> 167 us
  Pallas kernels: 0 us -> 59.3 us
  starting transfers between devices: 2.25 us -> 39.5 us
    reduce_scatter x14 -> x0, waiting for transfers between devices: 893 us -> none  [the longest x2 207 us: reduce_grads(): lax.psum_scatter(partials[6].astype(jnp.bfloat16), 'wide', scatter_dimens...]
    unnamed x41 -> x0, waiting for transfers between devices: 273 us -> none
    all_gather x5 -> x0, waiting for transfers between devices: 171 us -> none  [the longest x1 79.6 us: body(): lax.all_gather(columns[4], 'wide', axis=1, tiled=True)]
    ppermute x0 -> x48, waiting for transfers between devices: none -> 171 us  [shift(): return lax.ppermute(value, AXES, pairs)]
    dot_general x42 -> x12, matrix products: 167 us -> 29.5 us  [the longest x8 22.8 us: dot(): return lax.dot_general(a, b, dn, preferred_element_type=F32)]
    all_gather x9 -> x0, blocking collectives: 114 us -> none  [the longest x1 33.5 us: body(): lax.all_gather(columns[2], 'wide', axis=0, tiled=True)]
    pallas_call x0 -> x2, Pallas kernels: none -> 59.3 us  [ffn_call(): pl.pallas_call(functools.partial(ffn_kernel, tile), grid=(steps,), in_spe...]
    concatenate x0 -> x11, other arithmetic: none -> 53.9 us  [the longest x1 38.1 us: body(): jnp.concatenate([terms, gain_terms, spare], axis=4)]
  transfers between devices with their start and end apart: 30 -> 48, of which waited for: 28 -> 23; matrix products, arithmetic and copies ran while one was open for 11% -> 27% of each run, Pallas kernels for 0% -> 5%
where the time goes in v1:
time: 628 us; the launch traced here: 622 us
  waiting for transfers between devices  171 us (27%)
  local copies, waits for them, and re-layouts  167 us (27%)
  other arithmetic  120 us (19%)
  matrix products  61.1 us (10%)
  Pallas kernels  59.3 us (9%)
  starting transfers between devices  39.5 us (6%)
    ppermute x48, waiting for transfers between devices, shift(): return lax.ppermute(value, AXES, pairs)  171 us
    pallas_call x2, Pallas kernels, ffn_call(): pl.pallas_call(functools.partial(ffn_kernel, tile), grid=(steps,), in_spe...  59.3 us
    ppermute x48, starting transfers between devices, shift(): return lax.ppermute(value, AXES, pairs)  39.5 us
    concatenate x1, other arithmetic, body(): jnp.concatenate([terms, gain_terms, spare], axis=4)  38.1 us
    unnamed x379, local copies, waits for them, and re-layouts  37.5 us
    dynamic_slice x18, local copies, waits for them, and re-layouts, chosen(): return lax.dynamic_index_in_dim(array, index, 0, keepdims=False)  37.1 us
    reshape x6, local copies, waits for them, and re-layouts, blocked(): field.reshape(grid.outer, grid.inner, d_w, pair, 2, count)  33.6 us
    dot_general x8, matrix products, dot(): return lax.dot_general(a, b, dn, preferred_element_type=F32)  22.8 us
  transfers between devices with their start and end apart: 48, of which 23 were waited for; matrix products, arithmetic and copies ran while one was open for 27% of the time, Pallas kernels for 5%

profile of v1, /device:TPU:0, one launch (start us, length us, event | category | flops | bytes accessed | tf_op | source)
XLA Modules:
  0.0 621.6 jit_solution(16674401557827938029)
XLA Ops:
  39.2 9.2 %collective-permute-done.2 = bf16[128,640]{1,0:T(8,128)(2,1)S(1)} collective-permute-done((bf16[128,640]{1,0:T(8,128)(2,1)S(1)}, bf16[128,640]{1,0:T(8,128)(2,1)S(1)}, u32[]{:S(2)}, u32[]{:S(2)}) %collective-permute-start.2) | collective-permute-done | bytes 163872 | tf_op jit(solution)/shard_map/ppermute | solution.py:262
  56.4 8.0 %collective-permute-done.10 = bf16[3,160,256]{2,1,0:T(8,128)(2,1)S(1)} collective-permute-done((bf16[3,160,256]{2,1,0:T(8,128)(2,1)S(1)}, bf16[3,160,256]{2,1,0:T(8,128)(2,1)S(1)}, u32[]{:S(2)}, u32[]{:S(2)}) %collective-permute-start.10) | collective-permute-done | bytes 245792 | tf_op jit(solution)/shard_map/ppermute | solution.py:262
  72.3 16.9 %collective-permute-done.4 = bf16[2,4,64,640]{3,2,1,0:T(8,128)(2,1)S(1)} collective-permute-done((bf16[2,4,64,640]{3,2,1,0:T(8,128)(2,1)S(1)}, bf16[2,4,64,640]{3,2,1,0:T(8,128)(2,1)S(1)}, u32[]{:S(2)}, u32[]{:S(2)}) %collective-permute-start.4) | collective-permute-done | bytes 655392 | tf_op jit(solution)/shard_map/ppermute | solution.py:262
  100.6 9.6 %collective-permute-done.19 = bf16[4,3,96,256]{3,2,1,0:T(8,128)(2,1)S(1)} collective-permute-done((bf16[4,3,96,256]{3,2,1,0:T(8,128)(2,1)S(1)}, bf16[4,3,96,256]{3,2,1,0:T(8,128)(2,1)S(1)}, u32[]{:S(2)}, u32[]{:S(2)}) %collective-permute-start.19) | collective-permute-done | bytes 589856 | tf_op jit(solution)/shard_map/ppermute | solution.py:262
  130.4 4.0 maximum_maximum_fusion.1.own_ref
  134.4 9.2 %collective-permute-done.22 = bf16[2,4,3,64,256]{4,3,2,1,0:T(8,128)(2,1)} collective-permute-done((bf16[2,4,3,64,256]{4,3,2,1,0:T(8,128)(2,1)}, bf16[2,4,3,64,256]{4,3,2,1,0:T(8,128)(2,1)}, u32[]{:S(2)}, u32[]{:S(2)}) %collective-permute-start.22) | collective-permute-done | bytes 786464 | tf_op jit(solution)/shard_map/ppermute | solution.py:262
  143.6 6.3 %collective-permute-done.20 = bf16[8,3,96,256]{3,2,1,0:T(8,128)(2,1)} collective-permute-done((bf16[8,3,96,256]{3,2,1,0:T(8,128)(2,1)}, bf16[8,3,96,256]{3,2,1,0:T(8,128)(2,1)}, u32[]{:S(2)}, u32[]{:S(2)}) %collective-permute-start.20) | collective-permute-done | bytes 1179680 | tf_op jit(solution)/shard_map/ppermute | solution.py:262
  153.6 4.8 fusion.1
  176.7 6.5 %reshape.812 = bf16[960,960]{1,0:T(8,128)(2,1)S(1)} reshape(bf16[4,2,120,2,2,240]{5,4,3,2,1,0:T(2,128)(2,1)} %copy.239) | data formatting | bytes 3686400 | tf_op jit(solution)/shard_map/reshape | solution.py:383
  226.3 29.7 %feed_forward.2 = (bf16[2,8,3,160,256]{4,3,2,1,0:T(8,128)(2,1)}, bf16[2,8,3,160,256]{4,3,2,1,0:T(8,128)(2,1)}, f32[768,1024]{1,0:T(8,128)}, f32[768,1024]{1,0:T(8,128)}) custom-call(bf16[768,1024]{1,0:T(8,128)(2,1)} %multiply_convert_fusion.1.bf_ref, bf16[768,1024]{1,0:T(8,128)(2,1)} %fusion.8.gf_ref, ...), custom_call_target="tpu_custom_call" | custom-call | flops 18119393280 | bytes 25165824 | tf_op jit(solution)/shard_map/feed_forward/pallas_call | solution.py:223
  256.0 29.6 %feed_forward.3 = (bf16[2,8,3,160,256]{4,3,2,1,0:T(8,128)(2,1)}, bf16[2,8,3,160,256]{4,3,2,1,0:T(8,128)(2,1)}, f32[768,1024]{1,0:T(8,128)}, f32[768,1024]{1,0:T(8,128)}) custom-call(bf16[768,1024]{1,0:T(8,128)(2,1)} %multiply_convert_fusion.1.bf_ref, bf16[768,1024]{1,0:T(8,128)(2,1)} %fusion.8.gf_ref, ...), custom_call_target="tpu_custom_call" | custom-call | flops 18119393280 | bytes 25165824 | tf_op jit(solution)/shard_map/feed_forward/pallas_call | solution.py:223
  285.7 4.5 multiply_reduce_fusion
  290.7 4.8 multiply_add_fusion
  340.9 9.1 %reshape.861 = bf16[4,2,120,2,2,240]{5,4,3,2,1,0:T(2,128)(2,1)} reshape(bf16[960,960]{1,0:T(8,128)(2,1)} %convolution_convert_fusion.1) | data formatting | bytes 3686400 | tf_op jit(solution)/shard_map/reshape | solution.py:528
  354.7 9.6 %reshape.862 = bf16[4,2,120,2,2,240]{5,4,3,2,1,0:T(2,128)(2,1)} reshape(bf16[960,960]{1,0:T(8,128)(2,1)} %pad_maximum_fusion.4) | data formatting | bytes 3686400 | tf_op jit(solution)/shard_map/reshape | solution.py:528
  364.3 4.9 reshape.863
  369.1 5.7 copy.298
  390.5 6.3 %multiply_reduce_fusion.3 = (bf16[960]{0:T(1024)(128)(2,1)S(1)}, f32[768]{0:T(1024)S(1)}, f32[768,960]{0,1:T(8,128)}) fusion(bf16[768,960]{0,1:T(8,128)(2,1)S(1)} %bitcast.862, f32[768]{0:T(1024)S(1)} %copy-done.161, f32[960]{0:T(1024)S(1)} %copy-done.143, bf16[960,320]{0,1:T(8,128)(2,1)} %reshape.810, bf16[384,320]{0,1:T(8,128)(2,1)} %copy-done.133, ...), kind=kOutput, calls=%fused_computation.38 | convolution fusion | flops 479476032 | bytes 11439744 | tf_op jit(solution)/shard_map/dot_general | solution.py:167
  397.0 38.1 %maximum_maximum_fusion = bf16[2,2,2,4,128,640]{5,0,1,4,2,3:T(2,128)(2,1)S(1)} fusion(bf16[2,2,2,4,1,640]{5,0,1,4,2,3:T(2,128)(2,1)S(1)} %broadcast_in_dim.227, bf16[2,2,2,4,120,80]{5,0,1,4,2,3:T(2,128)(2,1)} %bitcast.875, bf16[2,2,2,4,120,80]{5,0,1,4,2,3:T(2,128)(2,1)} %bitcast.874, bf16[2,2,2,4,120,240]{5,0,1,4,2,3:T(2,128)(2,1)} %bitcast.867, ...), kind=kLoop, calls=%fused_computation.9 | loop fusion | flops 31457280 | bytes 10199296 | tf_op jit(solution)/shard_map/concatenate | solution.py:558
  435.2 12.0 %constant_dynamic-slice_fusion.1 = (bf16[1,2,2,4,128,640]{5,0,1,4,2,3:T(2,128)(2,1)}, bf16[1,2,2,4,128,640]{5,0,1,4,2,3:T(2,128)(2,1)S(1)}) fusion(bf16[2,2,2,4,128,640]{5,0,1,4,2,3:T(2,128)(2,1)S(1)} %maximum_maximum_fusion, s32[]{:T(128)S(6)} %select_n.366, s32[]{:T(128)S(6)} %select_n.365), kind=kLoop, calls=%fused_computation.528 | loop fusion | bytes 10485768 | tf_op jit(solution)/shard_map/jit(dynamic_index_in_dim)/dynamic_slice | solution.py:287
  465.0 11.8 %collective-permute-done.27 = bf16[2,4,64,640]{3,2,1,0:T(8,128)(2,1)S(1)} collective-permute-done((bf16[2,4,64,640]{3,2,1,0:T(8,128)(2,1)S(1)}, bf16[2,4,64,640]{3,2,1,0:T(8,128)(2,1)S(1)}, u32[]{:S(2)}, u32[]{:S(2)}) %collective-permute-start.27) | collective-permute-done | bytes 655392 | tf_op jit(solution)/shard_map/ppermute | solution.py:262
  495.8 7.1 %collective-permute-done.29 = bf16[128,640]{1,0:T(8,128)(2,1)S(1)} collective-permute-done((bf16[128,640]{1,0:T(8,128)(2,1)S(1)}, bf16[128,640]{1,0:T(8,128)(2,1)S(1)}, u32[]{:S(2)}, u32[]{:S(2)}) %collective-permute-start.29) | collective-permute-done | bytes 163872 | tf_op jit(solution)/shard_map/ppermute | solution.py:262
  522.4 12.4 %collective-permute-done.35 = bf16[2,4,3,64,256]{4,3,2,1,0:T(8,128)(2,1)S(1)} collective-permute-done((bf16[2,4,3,64,256]{4,3,2,1,0:T(8,128)(2,1)S(1)}, bf16[2,4,3,64,256]{4,3,2,1,0:T(8,128)(2,1)S(1)}, u32[]{:S(2)}, u32[]{:S(2)}) %collective-permute-start.35) | collective-permute-done | bytes 786464 | tf_op jit(solution)/shard_map/ppermute | solution.py:262
  535.5 12.7 %collective-permute-done.43 = bf16[2,4,3,64,256]{4,3,2,1,0:T(8,128)(2,1)S(1)} collective-permute-done((bf16[2,4,3,64,256]{4,3,2,1,0:T(8,128)(2,1)S(1)}, bf16[2,4,3,64,256]{4,3,2,1,0:T(8,128)(2,1)S(1)}, u32[]{:S(2)}, u32[]{:S(2)}) %collective-permute-start.43) | collective-permute-done | bytes 786464 | tf_op jit(solution)/shard_map/ppermute | solution.py:262
  551.0 23.6 %collective-permute-done.41 = bf16[8,3,96,256]{3,2,1,0:T(8,128)(2,1)S(1)} collective-permute-done((bf16[8,3,96,256]{3,2,1,0:T(8,128)(2,1)S(1)}, bf16[8,3,96,256]{3,2,1,0:T(8,128)(2,1)S(1)}, u32[]{:S(2)}, u32[]{:S(2)}) %collective-permute-start.41) | collective-permute-done | bytes 1179680 | tf_op jit(solution)/shard_map/ppermute | solution.py:262
  576.2 6.0 collective-permute-done.36
  582.3 4.2 collective-permute-done.44
  590.7 5.4 collective-permute-done.37
  596.3 5.0 collective-permute-done.45
  601.7 5.2 collective-permute-done.38
  607.0 5.1 collective-permute-done.46
  615.8 4.5 collective-permute-done.47
  (766 shorter events, 285.9 us)
Async XLA Ops:
  5.4 21.9 %collective-permute-start = (bf16[128,640]{1,0:T(8,128)(2,1)}, bf16[128,640]{1,0:T(8,128)(2,1)}, u32[]{:S(2)}, u32[]{:S(2)}) collective-permute-start(bf16[128,640]{1,0:T(8,128)(2,1)} %fusion.175), channel_id=1, source_target_pairs={{0,8},{1,9},{2,10},{3,11},{4,12},{5,13},{6,14},{7,15},{8,16},{9,17... | collective-permute-start | bytes 491528 | tf_op jit(solution)/shard_map/ppermute | solution.py:262
  10.5 16.7 %collective-permute-start.8 = (bf16[3,160,256]{2,1,0:T(8,128)(2,1)}, bf16[3,160,256]{2,1,0:T(8,128)(2,1)}, u32[]{:S(2)}, u32[]{:S(2)}) collective-permute-start(bf16[3,160,256]{2,1,0:T(8,128)(2,1)} %get-tuple-element.183), channel_id=1, source_target_pairs={{0,8},{1,9},{2,10},{3,11},{4,12},{5,13},{6,14},{7,15},{8,16},{9,17... | collective-permute-start | bytes 737288 | tf_op jit(solution)/shard_map/ppermute | solution.py:262
  12.1 17.9 %collective-permute-start.16 = (bf16[3,160,256]{2,1,0:T(8,128)(2,1)}, bf16[3,160,256]{2,1,0:T(8,128)(2,1)}, u32[]{:S(2)}, u32[]{:S(2)}) collective-permute-start(bf16[3,160,256]{2,1,0:T(8,128)(2,1)} %get-tuple-element.182), channel_id=1, source_target_pairs={{0,8},{1,9},{2,10},{3,11},{4,12},{5,13},{6,14},{7,15},{8,16},{9,17... | collective-permute-start | bytes 737288 | tf_op jit(solution)/shard_map/ppermute | solution.py:262
  27.3 27.3 %collective-permute-start.9 = (bf16[3,160,256]{2,1,0:T(8,128)(2,1)}, bf16[3,160,256]{2,1,0:T(8,128)(2,1)S(1)}, u32[]{:S(2)}, u32[]{:S(2)}) collective-permute-start(bf16[3,160,256]{2,1,0:T(8,128)(2,1)} %collective-permute-done.8), channel_id=1, source_target_pairs={{0,8},{1,9},{2,10},{3,11},{4,12},{5,13},{6,14},{7,15},{8,16},{9,17... | collective-permute-start | bytes 737288 | tf_op jit(solution)/shard_map/ppermute | solution.py:262
  30.0 24.6 %collective-permute-start.17 = (bf16[3,160,256]{2,1,0:T(8,128)(2,1)}, bf16[3,160,256]{2,1,0:T(8,128)(2,1)S(1)}, u32[]{:S(2)}, u32[]{:S(2)}) collective-permute-start(bf16[3,160,256]{2,1,0:T(8,128)(2,1)} %collective-permute-done.16), channel_id=1, source_target_pairs={{0,8},{1,9},{2,10},{3,11},{4,12},{5,13},{6,14},{7,15},{8,16},{9,17... | collective-permute-start | bytes 737288 | tf_op jit(solution)/shard_map/ppermute | solution.py:262
  51.5 15.5 %collective-permute-start.3 = (bf16[4,64,640]{2,1,0:T(8,128)(2,1)S(1)}, bf16[4,64,640]{2,1,0:T(8,128)(2,1)S(1)}, u32[]{:S(2)}, u32[]{:S(2)}) collective-permute-start(bf16[4,64,640]{2,1,0:T(8,128)(2,1)S(1)} %get-tuple-element.171), channel_id=1, source_target_pairs={{0,4},{1,5},{2,6},{3,7},{4,0},{5,1},{6,2},{7,3},{8,12},{9,13},{10,... | collective-permute-start | bytes 983048 | tf_op jit(solution)/shard_map/ppermute | solution.py:262
  53.1 14.9 %collective-permute-start.5 = (bf16[4,64,640]{2,1,0:T(8,128)(2,1)S(1)}, bf16[4,64,640]{2,1,0:T(8,128)(2,1)S(1)}, u32[]{:S(2)}, u32[]{:S(2)}) collective-permute-start(bf16[4,64,640]{2,1,0:T(8,128)(2,1)S(1)} %get-tuple-element.172), channel_id=1, source_target_pairs={{0,2},{1,3},{2,0},{3,1},{4,6},{5,7},{6,4},{7,5},{8,10},{9,11},{10,... | collective-permute-start | bytes 983048 | tf_op jit(solution)/shard_map/ppermute | solution.py:262
  64.5 32.8 %collective-permute-start.13 = (bf16[4,3,64,256]{3,2,1,0:T(8,128)(2,1)S(1)}, bf16[4,3,64,256]{3,2,1,0:T(8,128)(2,1)S(1)}, u32[]{:S(2)}, u32[]{:S(2)}) collective-permute-start(bf16[4,3,64,256]{3,2,1,0:T(8,128)(2,1)S(1)} %get-tuple-element.187), channel_id=1, source_target_pairs={{0,2},{1,3},{2,0},{3,1},{4,6},{5,7},{6,4},{7,5},{8,10},{9,11},{10,... | collective-permute-start | bytes 1179656 | tf_op jit(solution)/shard_map/ppermute | solution.py:262
  65.2 30.0 %collective-permute-start.11 = (bf16[4,3,96,256]{3,2,1,0:T(8,128)(2,1)S(1)}, bf16[4,3,96,256]{3,2,1,0:T(8,128)(2,1)S(1)}, u32[]{:S(2)}, u32[]{:S(2)}) collective-permute-start(bf16[4,3,96,256]{3,2,1,0:T(8,128)(2,1)S(1)} %pad_maximum_fusion.18), channel_id=1, source_target_pairs={{0,4},{1,5},{2,6},{3,7},{4,0},{5,1},{6,2},{7,3},{8,12},{9,13},{10,... | collective-permute-start | bytes 1769480 | tf_op jit(solution)/shard_map/ppermute | solution.py:262
  67.5 21.7 %collective-permute-start.4 = (bf16[2,4,64,640]{3,2,1,0:T(8,128)(2,1)S(1)}, bf16[2,4,64,640]{3,2,1,0:T(8,128)(2,1)S(1)}, u32[]{:S(2)}, u32[]{:S(2)}) collective-permute-start(bf16[2,4,64,640]{3,2,1,0:T(8,128)(2,1)S(1)} %fusion.145), channel_id=1, source_target_pairs={{0,2},{1,3},{2,0},{3,1},{4,6},{5,7},{6,4},{7,5},{8,10},{9,11},{10,... | collective-permute-start | bytes 1966088 | tf_op jit(solution)/shard_map/ppermute | solution.py:262
  68.4 21.5 %collective-permute-start.6 = (bf16[2,4,64,640]{3,2,1,0:T(8,128)(2,1)S(1)}, bf16[2,4,64,640]{3,2,1,0:T(8,128)(2,1)S(1)}, u32[]{:S(2)}, u32[]{:S(2)}) collective-permute-start(bf16[2,4,64,640]{3,2,1,0:T(8,128)(2,1)S(1)} %fusion.143), channel_id=1, source_target_pairs={{0,4},{1,5},{2,6},{3,7},{4,0},{5,1},{6,2},{7,3},{8,12},{9,13},{10,... | collective-permute-start | bytes 1966088 | tf_op jit(solution)/shard_map/ppermute | solution.py:262
  70.7 43.4 %collective-permute-start.21 = (bf16[4,3,64,256]{3,2,1,0:T(8,128)(2,1)}, bf16[4,3,64,256]{3,2,1,0:T(8,128)(2,1)}, u32[]{:S(2)}, u32[]{:S(2)}) collective-permute-start(bf16[4,3,64,256]{3,2,1,0:T(8,128)(2,1)} %get-tuple-element.185), channel_id=1, source_target_pairs={{0,2},{1,3},{2,0},{3,1},{4,6},{5,7},{6,4},{7,5},{8,10},{9,11},{10,... | collective-permute-start | bytes 1179656 | tf_op jit(solution)/shard_map/ppermute | solution.py:262
  93.9 59.7 %collective-permute-start.7 = (bf16[2,2,4,128,640]{4,3,2,1,0:T(8,128)(2,1)}, bf16[2,2,4,128,640]{4,3,2,1,0:T(8,128)(2,1)}, u32[]{:S(2)}, u32[]{:S(2)}) collective-permute-start(bf16[2,2,4,128,640]{4,3,2,1,0:T(8,128)(2,1)} %get-tuple-element.116), channel_id=1, source_target_pairs={{0,1},{1,0},{2,3},{3,2},{4,5},{5,4},{6,7},{7,6},{8,9},{9,8},{10,11... | collective-permute-start | bytes 7864328 | tf_op jit(solution)/shard_map/ppermute | solution.py:262
  94.0 16.2 %collective-permute-start.19 = (bf16[4,3,96,256]{3,2,1,0:T(8,128)(2,1)S(1)}, bf16[4,3,96,256]{3,2,1,0:T(8,128)(2,1)S(1)}, u32[]{:S(2)}, u32[]{:S(2)}) collective-permute-start(bf16[4,3,96,256]{3,2,1,0:T(8,128)(2,1)S(1)} %pad_maximum_fusion.19), channel_id=1, source_target_pairs={{0,4},{1,5},{2,6},{3,7},{4,0},{5,1},{6,2},{7,3},{8,12},{9,13},{10,... | collective-permute-start | bytes 1769480 | tf_op jit(solution)/shard_map/ppermute | solution.py:262
  96.1 34.3 %collective-permute-start.12 = (bf16[8,3,96,256]{3,2,1,0:T(8,128)(2,1)}, bf16[8,3,96,256]{3,2,1,0:T(8,128)(2,1)}, u32[]{:S(2)}, u32[]{:S(2)}) collective-permute-start(bf16[8,3,96,256]{3,2,1,0:T(8,128)(2,1)} %constant_dynamic-update-slice_fusion.10), channel_id=1, source_target_pairs={{0,2},{1,3},{2,0},{3,1},{4,6},{5,7},{6,4},{7,5},{8,10},{9,11},{10,... | collective-permute-start | bytes 3538952 | tf_op jit(solution)/shard_map/ppermute | solution.py:262
  99.1 31.3 %collective-permute-start.14 = (bf16[2,4,3,64,256]{4,3,2,1,0:T(8,128)(2,1)}, bf16[2,4,3,64,256]{4,3,2,1,0:T(8,128)(2,1)}, u32[]{:S(2)}, u32[]{:S(2)}) collective-permute-start(bf16[2,4,3,64,256]{4,3,2,1,0:T(8,128)(2,1)} %pad_maximum_fusion.16), channel_id=1, source_target_pairs={{0,4},{1,5},{2,6},{3,7},{4,0},{5,1},{6,2},{7,3},{8,12},{9,13},{10,... | collective-permute-start | bytes 2359304 | tf_op jit(solution)/shard_map/ppermute | solution.py:262
  111.0 38.9 %collective-permute-start.20 = (bf16[8,3,96,256]{3,2,1,0:T(8,128)(2,1)}, bf16[8,3,96,256]{3,2,1,0:T(8,128)(2,1)}, u32[]{:S(2)}, u32[]{:S(2)}) collective-permute-start(bf16[8,3,96,256]{3,2,1,0:T(8,128)(2,1)} %constant_dynamic-update-slice_fusion.15), channel_id=1, source_target_pairs={{0,2},{1,3},{2,0},{3,1},{4,6},{5,7},{6,4},{7,5},{8,10},{9,11},{10,... | collective-permute-start | bytes 3538952 | tf_op jit(solution)/shard_map/ppermute | solution.py:262
  116.1 27.5 %collective-permute-start.22 = (bf16[2,4,3,64,256]{4,3,2,1,0:T(8,128)(2,1)}, bf16[2,4,3,64,256]{4,3,2,1,0:T(8,128)(2,1)}, u32[]{:S(2)}, u32[]{:S(2)}) collective-permute-start(bf16[2,4,3,64,256]{4,3,2,1,0:T(8,128)(2,1)} %pad_maximum_fusion.17), channel_id=1, source_target_pairs={{0,4},{1,5},{2,6},{3,7},{4,0},{5,1},{6,2},{7,3},{8,12},{9,13},{10,... | collective-permute-start | bytes 2359304 | tf_op jit(solution)/shard_map/ppermute | solution.py:262
  134.4 91.9 %collective-permute-start.15 = (bf16[2,8,3,160,256]{4,3,2,1,0:T(8,128)(2,1)}, bf16[2,8,3,160,256]{4,3,2,1,0:T(8,128)(2,1)}, u32[]{:S(2)}, u32[]{:S(2)}) collective-permute-start(bf16[2,8,3,160,256]{4,3,2,1,0:T(8,128)(2,1)} %maximum_maximum_fusion.1.own_ref), channel_id=1, source_target_pairs={{0,1},{1,0},{2,3},{3,2},{4,5},{5,4},{6,7},{7,6},{8,9},{9,8},{10,11... | collective-permute-start | bytes 11796488 | tf_op jit(solution)/shard_map/ppermute | solution.py:262
  153.6 102.4 %collective-permute-start.23 = (bf16[2,8,3,160,256]{4,3,2,1,0:T(8,128)(2,1)}, bf16[2,8,3,160,256]{4,3,2,1,0:T(8,128)(2,1)}, u32[]{:S(2)}, u32[]{:S(2)}) collective-permute-start(bf16[2,8,3,160,256]{4,3,2,1,0:T(8,128)(2,1)} %maximum_maximum_fusion.2.own_ref), channel_id=1, source_target_pairs={{0,1},{1,0},{2,3},{3,2},{4,5},{5,4},{6,7},{7,6},{8,9},{9,8},{10,11... | collective-permute-start | bytes 11796488 | tf_op jit(solution)/shard_map/ppermute | solution.py:262
  450.7 59.7 %collective-permute-start.32 = (bf16[2,8,3,160,256]{4,3,2,1,0:T(8,128)(2,1)}, bf16[2,8,3,160,256]{4,3,2,1,0:T(8,128)(2,1)}, u32[]{:S(2)}, u32[]{:S(2)}) collective-permute-start(bf16[2,8,3,160,256]{4,3,2,1,0:T(8,128)(2,1)} %get-tuple-element.35), channel_id=1, source_target_pairs={{0,1},{1,0},{2,3},{3,2},{4,5},{5,4},{6,7},{7,6},{8,9},{9,8},{10,11... | collective-permute-start | bytes 11796488 | tf_op jit(solution)/shard_map/ppermute | solution.py:262
  450.7 65.1 %collective-permute-start.40 = (bf16[2,8,3,160,256]{4,3,2,1,0:T(8,128)(2,1)}, bf16[2,8,3,160,256]{4,3,2,1,0:T(8,128)(2,1)}, u32[]{:S(2)}, u32[]{:S(2)}) collective-permute-start(bf16[2,8,3,160,256]{4,3,2,1,0:T(8,128)(2,1)} %get-tuple-element.37), channel_id=1, source_target_pairs={{0,1},{1,0},{2,3},{3,2},{4,5},{5,4},{6,7},{7,6},{8,9},{9,8},{10,11... | collective-permute-start | bytes 11796488 | tf_op jit(solution)/shard_map/ppermute | solution.py:262
  460.0 16.8 %collective-permute-start.27 = (bf16[2,4,64,640]{3,2,1,0:T(8,128)(2,1)S(1)}, bf16[2,4,64,640]{3,2,1,0:T(8,128)(2,1)S(1)}, u32[]{:S(2)}, u32[]{:S(2)}) collective-permute-start(bf16[2,4,64,640]{3,2,1,0:T(8,128)(2,1)S(1)} %dynamic-slice_bitcast_fusion.4), channel_id=1, source_target_pairs={{0,4},{1,5},{2,6},{3,7},{4,0},{5,1},{6,2},{7,3},{8,12},{9,13},{10,... | collective-permute-start | bytes 1966088 | tf_op jit(solution)/shard_map/ppermute | solution.py:262
  463.9 17.0 %collective-permute-start.25 = (bf16[2,4,64,640]{3,2,1,0:T(8,128)(2,1)S(1)}, bf16[2,4,64,640]{3,2,1,0:T(8,128)(2,1)S(1)}, u32[]{:S(2)}, u32[]{:S(2)}) collective-permute-start(bf16[2,4,64,640]{3,2,1,0:T(8,128)(2,1)S(1)} %dynamic-slice_bitcast_fusion.5), channel_id=1, source_target_pairs={{0,2},{1,3},{2,0},{3,1},{4,6},{5,7},{6,4},{7,5},{8,10},{9,11},{10,... | collective-permute-start | bytes 1966088 | tf_op jit(solution)/shard_map/ppermute | solution.py:262
  477.7 15.7 %collective-permute-start.28 = (bf16[4,64,640]{2,1,0:T(8,128)(2,1)}, bf16[4,64,640]{2,1,0:T(8,128)(2,1)S(1)}, u32[]{:S(2)}, u32[]{:S(2)}) collective-permute-start(bf16[4,64,640]{2,1,0:T(8,128)(2,1)} %dynamic-slice_bitcast_fusion.10), channel_id=1, source_target_pairs={{0,2},{1,3},{2,0},{3,1},{4,6},{5,7},{6,4},{7,5},{8,10},{9,11},{10,... | collective-permute-start | bytes 983048 | tf_op jit(solution)/shard_map/ppermute | solution.py:262
  514.3 20.5 %collective-permute-start.35 = (bf16[2,4,3,64,256]{4,3,2,1,0:T(8,128)(2,1)S(1)}, bf16[2,4,3,64,256]{4,3,2,1,0:T(8,128)(2,1)S(1)}, u32[]{:S(2)}, u32[]{:S(2)}) collective-permute-start(bf16[2,4,3,64,256]{4,3,2,1,0:T(8,128)(2,1)S(1)} %slice.809), channel_id=1, source_target_pairs={{0,4},{1,5},{2,6},{3,7},{4,0},{5,1},{6,2},{7,3},{8,12},{9,13},{10,... | collective-permute-start | bytes 2359304 | tf_op jit(solution)/shard_map/ppermute | solution.py:262
  519.5 28.7 %collective-permute-start.43 = (bf16[2,4,3,64,256]{4,3,2,1,0:T(8,128)(2,1)S(1)}, bf16[2,4,3,64,256]{4,3,2,1,0:T(8,128)(2,1)S(1)}, u32[]{:S(2)}, u32[]{:S(2)}) collective-permute-start(bf16[2,4,3,64,256]{4,3,2,1,0:T(8,128)(2,1)S(1)} %slice.823), channel_id=1, source_target_pairs={{0,4},{1,5},{2,6},{3,7},{4,0},{5,1},{6,2},{7,3},{8,12},{9,13},{10,... | collective-permute-start | bytes 2359304 | tf_op jit(solution)/shard_map/ppermute | solution.py:262
  520.3 29.0 %collective-permute-start.33 = (bf16[8,3,96,256]{3,2,1,0:T(8,128)(2,1)S(1)}, bf16[8,3,96,256]{3,2,1,0:T(8,128)(2,1)S(1)}, u32[]{:S(2)}, u32[]{:S(2)}) collective-permute-start(bf16[8,3,96,256]{3,2,1,0:T(8,128)(2,1)S(1)} %slice_bitcast_fusion.4), channel_id=1, source_target_pairs={{0,2},{1,3},{2,0},{3,1},{4,6},{5,7},{6,4},{7,5},{8,10},{9,11},{10,... | collective-permute-start | bytes 3538952 | tf_op jit(solution)/shard_map/ppermute | solution.py:262
  520.8 53.7 %collective-permute-start.41 = (bf16[8,3,96,256]{3,2,1,0:T(8,128)(2,1)S(1)}, bf16[8,3,96,256]{3,2,1,0:T(8,128)(2,1)S(1)}, u32[]{:S(2)}, u32[]{:S(2)}) collective-permute-start(bf16[8,3,96,256]{3,2,1,0:T(8,128)(2,1)S(1)} %slice_bitcast_fusion.2), channel_id=1, source_target_pairs={{0,2},{1,3},{2,0},{3,1},{4,6},{5,7},{6,4},{7,5},{8,10},{9,11},{10,... | collective-permute-start | bytes 3538952 | tf_op jit(solution)/shard_map/ppermute | solution.py:262
  534.9 47.3 %collective-permute-start.36 = (bf16[4,3,64,256]{3,2,1,0:T(8,128)(2,1)S(1)}, bf16[4,3,64,256]{3,2,1,0:T(8,128)(2,1)S(1)}, u32[]{:S(2)}, u32[]{:S(2)}) collective-permute-start(bf16[4,3,64,256]{3,2,1,0:T(8,128)(2,1)S(1)} %slice_bitcast_fusion.22), channel_id=1, source_target_pairs={{0,2},{1,3},{2,0},{3,1},{4,6},{5,7},{6,4},{7,5},{8,10},{9,11},{10,... | collective-permute-start | bytes 1179656 | tf_op jit(solution)/shard_map/ppermute | solution.py:262
  548.4 38.1 %collective-permute-start.44 = (bf16[4,3,64,256]{3,2,1,0:T(8,128)(2,1)S(1)}, bf16[4,3,64,256]{3,2,1,0:T(8,128)(2,1)S(1)}, u32[]{:S(2)}, u32[]{:S(2)}) collective-permute-start(bf16[4,3,64,256]{3,2,1,0:T(8,128)(2,1)S(1)} %slice_bitcast_fusion.20), channel_id=1, source_target_pairs={{0,2},{1,3},{2,0},{3,1},{4,6},{5,7},{6,4},{7,5},{8,10},{9,11},{10,... | collective-permute-start | bytes 1179656 | tf_op jit(solution)/shard_map/ppermute | solution.py:262
  549.4 37.1 %collective-permute-start.34 = (bf16[4,3,96,256]{3,2,1,0:T(8,128)(2,1)S(1)}, bf16[4,3,96,256]{3,2,1,0:T(8,128)(2,1)S(1)}, u32[]{:S(2)}, u32[]{:S(2)}) collective-permute-start(bf16[4,3,96,256]{3,2,1,0:T(8,128)(2,1)S(1)} %slice.807), channel_id=1, source_target_pairs={{0,4},{1,5},{2,6},{3,7},{4,0},{5,1},{6,2},{7,3},{8,12},{9,13},{10,... | collective-permute-start | bytes 1769480 | tf_op jit(solution)/shard_map/ppermute | solution.py:262
  (189 other events, 1614.7 us)
